TPU v7x, 256 devices: a whole 4x4x8 slice. The times are simulated.
256 devices in a mesh: span: 32 (over x, y, core), band: 8 (over z).
Axes of the slice: x: 4, y: 4, z: 8, core: 2. Of those that a mesh axis runs over, the one named last changes fastest.
Arguments:
- start_block: float32 [524288, 128], P(('span', 'band')), may hold values from -500 to 500
- diagonal: float32 [524288], P(('span', 'band')), may hold values from 0.5 to 2
- blocks: bfloat16 [2048, 8, 256, 256], P(('span', 'band')), may hold values from -0.25 to 0.25
- span_offsets: int32 [2048, 8], P(('span', 'band')), may hold values from -1 to 1, as said below
- col_offsets: int32 [2048, 8], P(('span', 'band')), may hold values from -2 to 2
Outputs:
- bases_out: float32 [3, 524288, 128], P(None, ('span', 'band'))
- hessenberg: float32 [512, 384], replicated
- r_first: float32 [128, 128], replicated
Inputs may be any that keep to these rules, and one draw needn't show every extreme that they name: The 8 pairs (span_offsets, col_offsets) of one block row are different from each other.
All inputs are finite; a program needn't handle non-finite values.
Results may differ from a plain program's by a relative error of at most 0.0029.
The roundings to bfloat16 on the way count: a program that leaves them out, or rounds other values in their place, can miss the bound.
Values may be sent and summed in bfloat16 or wider, within the bound.
A program may use at most 128 MiB of HBM per device.

v0:
```python
import jax
import jax.numpy as jnp
from jax import lax
from jax.sharding import PartitionSpec as P

W = 2
STEPS = 3


def padded(block, sides, width):
    for axis, dim in sides:
        count = lax.axis_size(axis)
        forward = [(i, i + 1) for i in range(count - 1)]
        backward = [(target, source) for source, target in forward]
        low = lax.ppermute(
            lax.slice_in_dim(block, block.shape[dim] - width, None, axis=dim), axis, forward
        )
        high = lax.ppermute(lax.slice_in_dim(block, 0, width, axis=dim), axis, backward)
        block = jnp.concatenate([low, block, high], axis=dim)
    return block


def local_inner(first, second, row_total):
    return (
        jnp.dot(
            first.T, second, precision=lax.Precision.HIGHEST, preferred_element_type=jnp.float32
        )
        / row_total
    )


def from_upper(upper_fac, matrix):
    identity = jnp.eye(upper_fac.shape[0], dtype=jnp.float32)
    inverse = jax.scipy.linalg.solve_triangular(upper_fac.T, identity, lower=True)
    return jnp.dot(
        matrix, inverse.T, precision=lax.Precision.HIGHEST, preferred_element_type=jnp.float32
    )


def from_gram(gram_mat, matrix):
    upper_fac = jnp.linalg.cholesky(gram_mat).T
    return (upper_fac, from_upper(upper_fac, matrix))


def apply_operator(vector, diagonal, blocks, span_offsets, col_offsets):
    block_count = blocks.shape[0]
    block_size = blocks.shape[2]
    vec_width = vector.shape[1]
    lowered = vector.astype(jnp.bfloat16).reshape(1, block_count, block_size * vec_width)
    face_cells = padded(lowered, (("span", 0),), 1)
    extended = padded(face_cells, (("band", 1),), W)
    stride = block_count + 2 * W
    lookup = extended.reshape(3 * stride, block_size, vec_width)
    row_ids = jnp.arange(block_count, dtype=jnp.int32)[:, None]
    flat_index = (span_offsets + 1) * stride + row_ids + W + col_offsets
    picked = jnp.take(lookup, flat_index, axis=0)
    coupled = jnp.einsum("ikab,ikbc->iac", blocks, picked, preferred_element_type=jnp.float32)
    return diagonal[:, None] * vector + coupled.reshape(block_count * block_size, vec_width)


def subtract_projections(mapped, bases, coeffs):
    residual = mapped
    for position in range(len(bases)):
        residual = residual - jnp.dot(
            bases[position],
            coeffs[position],
            precision=lax.Precision.HIGHEST,
            preferred_element_type=jnp.float32,
        )
    return residual


def per_device(start_block, diagonal, blocks, span_offsets, col_offsets):
    row_total = float(start_block.shape[0] * lax.axis_size("span") * lax.axis_size("band"))
    vec_width = start_block.shape[1]
    first_gram = lax.psum(local_inner(start_block, start_block, row_total), ("span", "band"))
    r_first, current = from_gram(first_gram, start_block)
    bases = [current]
    columns = []
    for step_id in range(STEPS):
        mapped = apply_operator(bases[-1], diagonal, blocks, span_offsets, col_offsets)
        partials = jnp.stack([local_inner(earlier, mapped, row_total) for earlier in bases])
        coeffs = lax.psum(partials, ("span", "band"))
        residual = subtract_projections(mapped, bases, coeffs)
        gram_mat = lax.psum(local_inner(residual, residual, row_total), ("span", "band"))
        r_next, q_next = from_gram(gram_mat, residual)
        pieces = [coeffs.reshape(len(bases) * vec_width, vec_width), r_next]
        if STEPS - 1 - step_id > 0:
            pieces.append(jnp.zeros(((STEPS - 1 - step_id) * vec_width, vec_width), jnp.float32))
        columns.append(jnp.concatenate(pieces, axis=0))
        bases.append(q_next)
    hessenberg = jnp.concatenate(columns, axis=1)
    bases_out = jnp.stack(bases[1:])
    return (bases_out, hessenberg, r_first)


def solution(mesh):
    placed = (
        P(("span", "band"), None),
        P(("span", "band")),
        P(("span", "band"), None, None, None),
        P(("span", "band"), None),
        P(("span", "band"), None),
    )
    return jax.shard_map(
        per_device,
        mesh=mesh,
        in_specs=placed,
        out_specs=(P(None, ("span", "band"), None), P(), P()),
        check_vma=False,
    )
```

profile of v0, /device:TPU:1, one launch (start us, length us, event | category | flops | bytes accessed | tf_op | source)
XLA Modules:
  0.0 2016.5 jit_solution(8511894342165409740)
XLA Ops:
  8.4 2.4 convolution_multiply_fusion.9
  10.9 245.1 %all-reduce.8.cloned.1.call-done = f32[128,128]{0,1:T(8,128)} async-done(((f32[128,128]{0,1:T(8,128)}), f32[128,128]{0,1:T(8,128)}) %all-reduce.8.cloned.1.call-update) | async-done | bytes 65552 | tf_op jit(solution)/shard_map/psum | solution.py:76
  257.8 11.7 cholesky.74
  270.9 9.8 custom-call.8
  282.6 2.6 collective-permute-start
  285.2 1.9 collective-permute-start.1
  287.1 4.2 collective-permute-done
  291.4 4.3 collective-permute-done.1
  297.4 3.2 collective-permute-start.2
  302.5 2.8 collective-permute-done.2
  305.3 3.8 collective-permute-done.3
  309.2 4.5 pad_maximum_fusion
  313.7 4.9 reshape.55
  318.6 4.7 gather_fusion
  323.3 6.5 copy.34
  329.8 7.5 fusion.12
  339.2 239.2 %all-reduce.10.cloned.1.call-done = f32[128,128]{0,1:T(8,128)} async-done(((f32[128,128]{0,1:T(8,128)}), f32[128,128]{0,1:T(8,128)}) %all-reduce.10.cloned.1.call-update) | async-done | bytes 65552 | tf_op jit(solution)/shard_map/psum | solution.py:83
  578.4 2.0 convolution_subtract_fusion.5
  582.2 236.3 %all-reduce.12.cloned.1.call-done = f32[128,128]{0,1:T(8,128)} async-done(((f32[128,128]{0,1:T(8,128)}), f32[128,128]{0,1:T(8,128)}) %all-reduce.12.cloned.1.call-update) | async-done | bytes 65552 | tf_op jit(solution)/shard_map/psum | solution.py:85
  820.4 11.7 cholesky.85
  834.0 9.8 custom-call.9
  844.2 2.6 fusion.54
  848.0 2.6 collective-permute-start.4
  850.6 1.9 collective-permute-start.5
  852.5 4.2 collective-permute-done.4
  856.8 4.3 collective-permute-done.5
  861.7 3.5 collective-permute-start.6
  866.7 3.2 collective-permute-done.6
  869.9 3.8 collective-permute-done.7
  873.7 3.1 pad_maximum_fusion.1
  876.8 4.9 reshape.58
  881.7 4.7 gather_fusion.1
  886.4 6.5 copy.40
  892.9 7.5 fusion.15
  908.1 241.3 %all-reduce.14.cloned.1.call-done = f32[2,128,128]{1,2,0:T(8,128)} async-done(((f32[2,128,128]{1,2,0:T(8,128)}), f32[2,128,128]{1,2,0:T(8,128)}) %all-reduce.14.cloned.1.call-update) | async-done | bytes 131088 | tf_op jit(solution)/shard_map/psum | solution.py:83
  1149.4 2.7 convolution_subtract_fusion.4
  1153.1 2.4 convolution_multiply_fusion.4
  1155.6 235.9 %all-reduce.16.cloned.1.call-done = f32[128,128]{0,1:T(8,128)} async-done(((f32[128,128]{0,1:T(8,128)}), f32[128,128]{0,1:T(8,128)}) %all-reduce.16.cloned.1.call-update) | async-done | bytes 65552 | tf_op jit(solution)/shard_map/psum | solution.py:85
  1393.3 11.7 cholesky.96
  1406.9 9.8 custom-call.10
  1417.1 3.0 fusion.55
  1420.1 2.4 reshape.60
  1422.5 2.6 collective-permute-start.8
  1425.1 1.9 collective-permute-start.9
  1427.0 4.5 collective-permute-done.8
  1432.6 3.2 collective-permute-done.9
  1436.3 3.5 collective-permute-start.10
  1441.3 3.2 collective-permute-done.10
  1444.5 3.8 collective-permute-done.11
  1448.4 3.1 pad_maximum_fusion.2
  1451.5 4.9 reshape.61
  1456.4 4.7 gather_fusion.2
  1461.1 6.5 copy.46
  1467.6 8.5 fusion.18
  1476.1 2.5 copy.47
  1482.0 1.9 fusion.22
  1483.9 1.9 fusion.21
  1486.8 246.8 %all-reduce.18.cloned.1.call-done = f32[3,128,128]{1,2,0:T(8,128)} async-done(((f32[3,128,128]{1,2,0:T(8,128)}), f32[3,128,128]{1,2,0:T(8,128)}) %all-reduce.18.cloned.1.call-update) | async-done | bytes 196624 | tf_op jit(solution)/shard_map/psum | solution.py:83
  1733.6 3.1 convolution_subtract_fusion.2
  1739.7 2.4 convolution_multiply_fusion
  1748.4 230.6 %all-reduce.20.cloned.1.call-done = f32[128,128]{0,1:T(8,128)} async-done(((f32[128,128]{0,1:T(8,128)}), f32[128,128]{0,1:T(8,128)}) %all-reduce.20.cloned.1.call-update) | async-done | bytes 65552 | tf_op jit(solution)/shard_map/psum | solution.py:85
  1980.8 11.7 cholesky.107
  1994.1 9.8 custom-call.11
  2004.2 2.2 convolution_bitcast_fusion
  (120 shorter events, 56.9 us)
Async XLA Ops:
  7.2 1.2 copy-start
  7.2 248.8 %all-reduce.8.cloned.1.call-start = ((), (), s32[]{:S(2)}) async-start(), calls=%async_computation | async-start | bytes 131072 | tf_op jit(solution)/shard_map/psum | solution.py:76
  10.9 567.5 %all-reduce.10.cloned.1.call-start = ((), (), s32[]{:S(2)}) async-start(), calls=%async_computation.1 | async-start | bytes 131072 | tf_op jit(solution)/shard_map/psum | solution.py:83
  282.3 20.1 copy-start.15
  282.4 20.1 copy-start.16
  282.6 8.7 collective-permute-start
  285.2 10.5 collective-permute-start.1
  295.7 1.2 copy-start.7
  297.4 7.9 collective-permute-start.2
  300.6 8.5 collective-permute-start.3
  329.8 7.6 copy-start.14
  339.1 479.5 %all-reduce.12.cloned.1.call-start = ((), (), s32[]{:S(2)}) async-start(), calls=%async_computation.2 | async-start | bytes 131072 | tf_op jit(solution)/shard_map/psum | solution.py:85
  582.0 567.3 %all-reduce.14.cloned.1.call-start = ((), (), s32[]{:S(2)}) async-start(), calls=%async_computation.3 | async-start | bytes 262144 | tf_op jit(solution)/shard_map/psum | solution.py:83
  848.0 8.7 collective-permute-start.4
  850.6 10.5 collective-permute-start.5
  861.7 8.2 collective-permute-start.6
  865.2 8.5 collective-permute-start.7
  907.6 483.9 %all-reduce.16.cloned.1.call-start = ((), (), s32[]{:S(2)}) async-start(), calls=%async_computation.4 | async-start | bytes 131072 | tf_op jit(solution)/shard_map/psum | solution.py:85
  1149.4 2.7 copy-start.9
  1153.1 263.7 %copy-start.6 = (f32[2048,128]{1,0:T(8,128)}, f32[2048,128]{1,0:T(8,128)S(1)}, u32[]{:S(2)}) copy-start(f32[2048,128]{1,0:T(8,128)S(1)} %convolution_subtract_fusion.3) | copy-start | bytes 3145732
  1155.6 578.0 %all-reduce.18.cloned.1.call-start = ((), (), s32[]{:S(2)}) async-start(), calls=%async_computation.5 | async-start | bytes 393216 | tf_op jit(solution)/shard_map/psum | solution.py:83
  1420.1 317.6 %copy-start.2 = (f32[2048,128]{1,0:T(8,128)}, f32[2048,128]{1,0:T(8,128)S(1)}, u32[]{:S(2)}) copy-start(f32[2048,128]{1,0:T(8,128)S(1)} %get-tuple-element.31) | copy-start | bytes 3145732
  1422.5 9.0 collective-permute-start.8
  1425.1 10.7 collective-permute-start.9
  1436.3 8.2 collective-permute-start.10
  1439.9 8.5 collective-permute-start.11
  1480.2 5.6 copy-start.4
  1486.5 492.5 %all-reduce.20.cloned.1.call-start = ((), (), s32[]{:S(2)}) async-start(), calls=%async_computation.6 | async-start | bytes 131072 | tf_op jit(solution)/shard_map/psum | solution.py:85
  1733.6 3.1 copy-start.8
  1738.7 1.0 copy-start.5
  1739.7 266.8 %copy-start.3 = (f32[2048,128]{1,0:T(8,128)S(1)}, f32[2048,128]{1,0:T(8,128)}, u32[]{:S(2)}) copy-start(f32[2048,128]{1,0:T(8,128)} %copy-done.2) | copy-start | bytes 3145732
  2006.4 2.9 copy-start.1
  2006.5 1.9 copy-start.10
  2006.5 1.9 copy-start.11
  2006.5 1.9 copy-start.12
  2006.5 1.9 copy-start.13
Sparse Core Ops, SparseCore 0:
  14.1 241.8 all-reduce.7
  339.3 239.1 all-reduce.9
  584.5 234.0 all-reduce.11
  907.7 241.5 all-reduce.13
  1155.7 235.7 all-reduce.15
  1486.6 246.8 all-reduce.17
  1742.2 236.7 all-reduce.19
where the time goes:
time: 2030 us; the launch traced here: 2020 us
  waiting for transfers between devices  1720 us (85%)
  other arithmetic  114 us (6%)
  local copies, waits for them, and re-layouts  72.9 us (4%)
  matrix products  64.1 us (3%)
  starting transfers between devices  29.6 us (1%)
    psum x3, waiting for transfers between devices, per_device(): coeffs = lax.psum(partials, ('span', 'band'))  727 us
    psum x3, waiting for transfers between devices, per_device(): lax.psum(local_inner(residual, residual, row_total), ('span', 'band'))  703 us
    psum x1, waiting for transfers between devices, per_device(): lax.psum(local_inner(start_block, start_block, row_total), ('span', 'band'))  245 us
    another operation x12, other arithmetic, from_gram(): upper_fac = jnp.linalg.cholesky(gram_mat).T  49.6 us
  transfers between devices with their start and end apart: 19, of which 19 were waited for; matrix products, arithmetic and copies ran while one was open for 0% of the time, Pallas kernels for 0%

commit v1 on v0

--- a/solution.py
+++ b/solution.py
@@ -1,10 +1,17 @@
 import jax
 import jax.numpy as jnp
 from jax import lax
+from jax.experimental import pallas as pl
+from jax.experimental.pallas import tpu as pltpu
 from jax.sharding import PartitionSpec as P
 
 W = 2
 STEPS = 3
+LIMIT = 16384.0
+F32 = jnp.float32
+BF16 = jnp.bfloat16
+MESH = pl.DeviceIdType.MESH
+HIGHEST = lax.Precision.HIGHEST
 
 
 def padded(block, sides, width):
@@ -22,19 +29,14 @@
 
 def local_inner(first, second, row_total):
     return (
-        jnp.dot(
-            first.T, second, precision=lax.Precision.HIGHEST, preferred_element_type=jnp.float32
-        )
-        / row_total
+        jnp.dot(first.T, second, precision=HIGHEST, preferred_element_type=jnp.float32) / row_total
     )
 
 
 def from_upper(upper_fac, matrix):
     identity = jnp.eye(upper_fac.shape[0], dtype=jnp.float32)
     inverse = jax.scipy.linalg.solve_triangular(upper_fac.T, identity, lower=True)
-    return jnp.dot(
-        matrix, inverse.T, precision=lax.Precision.HIGHEST, preferred_element_type=jnp.float32
-    )
+    return jnp.dot(matrix, inverse.T, precision=HIGHEST, preferred_element_type=jnp.float32)
 
 
 def from_gram(gram_mat, matrix):
@@ -64,13 +66,13 @@
         residual = residual - jnp.dot(
             bases[position],
             coeffs[position],
-            precision=lax.Precision.HIGHEST,
+            precision=HIGHEST,
             preferred_element_type=jnp.float32,
         )
     return residual
 
 
-def per_device(start_block, diagonal, blocks, span_offsets, col_offsets):
+def plain_form(start_block, diagonal, blocks, span_offsets, col_offsets):
     row_total = float(start_block.shape[0] * lax.axis_size("span") * lax.axis_size("band"))
     vec_width = start_block.shape[1]
     first_gram = lax.psum(local_inner(start_block, start_block, row_total), ("span", "band"))
@@ -94,6 +96,446 @@
     return (bases_out, hessenberg, r_first)
 
 
+def dot(a, b):
+    return jnp.dot(a, b, preferred_element_type=F32)
+
+
+def dot_rows(a, b, precision=None):
+    return lax.dot_general(
+        a, b, (((0,), (0,)), ((), ())), precision=precision, preferred_element_type=F32
+    )
+
+
+def split2(x):
+    high = x.astype(BF16)
+    return high, (x - high.astype(F32)).astype(BF16)
+
+
+def both(x):
+    return jnp.concatenate(split2(x), axis=1)
+
+
+def square(x):
+    pair = both(x)
+    return jnp.concatenate([pair, pair], axis=0)
+
+
+def halves(x):
+    n = x.shape[1] // 2
+    return x[:, :n] + x[:, n:]
+
+
+def quarters(x):
+    n = x.shape[0] // 2
+    return halves(x[:n] + x[n:])
+
+
+def kernel(
+    dims,
+    start_ref,
+    diag_ref,
+    blocks_ref,
+    spans_ref,
+    cols_ref,
+    bases_ref,
+    hess_ref,
+    first_ref,
+    flag_ref,
+    blk,
+    ext,
+    qf,
+    qs,
+    mf,
+    dg,
+    gram,
+    work,
+    fac,
+    inv,
+    hb,
+    lb,
+    part,
+    recv1,
+    mid,
+    recv2,
+    fin,
+    total,
+    cond,
+    send_sem,
+    recv_sem,
+    halo_send,
+    halo_recv,
+    blk_sem,
+    out_sem,
+):
+    n_span, n_band, nb, bs, width, kc = dims
+    n_xy, n_zc = n_span // 2, n_band * 2
+    rows = nb * bs
+    stride = nb + 2 * W
+    chunk = width // n_xy
+    scale = 1.0 / (rows * n_span * n_band)
+    s = lax.axis_index("span")
+    z = lax.axis_index("band")
+    xy, core = s // 2, s % 2
+    zc = z * 2 + core
+
+    def xy_peer(d):
+        peer = lax.rem(xy + d, n_xy)
+        return peer, (peer * 2 + core, z)
+
+    def zc_peer(d):
+        peer = lax.rem(zc + d, n_zc)
+        return peer, (xy * 2 + lax.rem(peer, 2), peer // 2)
+
+    ways = [(ds, db) for db in (0, -1, 1) for ds in (-1, 0, 1) if (ds, db) != (0, 0)]
+
+    def reaches(ds, db):
+        return (s + ds >= 0) & (s + ds < n_span) & (z + db >= 0) & (z + db < n_band)
+
+    def halo_copy(n):
+        ds, db = ways[n]
+        seg = (1 - ds) * stride
+        if db == 0:
+            source, target, count = W, W, nb
+        elif db == 1:
+            source, target, count = nb, 0, W
+        else:
+            source, target, count = W, nb + W, W
+        return pltpu.make_async_remote_copy(
+            src_ref=ext.at[pl.ds(stride + source, count)],
+            dst_ref=ext.at[pl.ds(seg + target, count)],
+            send_sem=halo_send.at[n],
+            recv_sem=halo_recv.at[n],
+            device_id=(s + ds, z + db),
+            device_id_type=MESH,
+        )
+
+    load = pltpu.make_async_copy(blocks_ref, blk, blk_sem)
+    load.start()
+    ext[...] = jnp.zeros_like(ext)
+    barrier = pltpu.get_barrier_semaphore()
+
+    def greet(peer_of):
+        def body(d, carry):
+            pl.semaphore_signal(barrier, inc=1, device_id=peer_of(d)[1], device_id_type=MESH)
+            return carry
+
+        return body
+
+    lax.fori_loop(1, n_xy, greet(xy_peer), 0)
+    lax.fori_loop(1, n_zc, greet(zc_peer), 0)
+    for ds, db in ways:
+
+        @pl.when(reaches(ds, db))
+        def _():
+            pl.semaphore_signal(barrier, inc=1, device_id=(s + ds, z + db), device_id_type=MESH)
+
+    def accumulate(lefts, right):
+        for m, left in enumerate(lefts):
+            gram[m] = gram[m] + dot_rows(left, right)
+
+    def publish(t, nm):
+        for m in range(nm):
+            part[t, :, m] = (quarters(gram[m]) * scale).reshape(n_xy, chunk, width)
+
+    def all_reduce(t, nm, meanwhile=None):
+        take = pl.ds(0, nm)
+        par = t % 2
+
+        def first(d):
+            peer, device = xy_peer(d)
+            return pltpu.make_async_remote_copy(
+                src_ref=part.at[t, peer, take],
+                dst_ref=recv1.at[t, xy, take],
+                send_sem=send_sem.at[0, peer],
+                recv_sem=recv_sem.at[par, 0, xy],
+                device_id=device,
+                device_id_type=MESH,
+            )
+
+        def second(d):
+            peer, device = zc_peer(d)
+            return pltpu.make_async_remote_copy(
+                src_ref=mid.at[t, take],
+                dst_ref=recv2.at[t, zc, take],
+                send_sem=send_sem.at[1, peer],
+                recv_sem=recv_sem.at[par, 1, zc],
+                device_id=device,
+                device_id_type=MESH,
+            )
+
+        def third(d):
+            peer, device = xy_peer(d)
+            return pltpu.make_async_remote_copy(
+                src_ref=fin.at[t, take],
+                dst_ref=total.at[t, xy, take],
+                send_sem=send_sem.at[2, peer],
+                recv_sem=recv_sem.at[par, 2, xy],
+                device_id=device,
+                device_id_type=MESH,
+            )
+
+        def landed(buffer, stage, who, like):
+            peer, device = who
+            pltpu.make_async_remote_copy(
+                src_ref=like,
+                dst_ref=buffer.at[t, peer, take],
+                send_sem=send_sem.at[stage, peer],
+                recv_sem=recv_sem.at[par, stage, peer],
+                device_id=device,
+                device_id_type=MESH,
+            ).wait_recv()
+
+        def each(n, act):
+            def body(d, carry):
+                act(d)
+                return carry
+
+            lax.fori_loop(1, n, body, 0)
+
+        each(n_xy, lambda d: first(d).start())
+        recv1[t, xy, :nm] = part[t, xy, :nm]
+        if meanwhile is not None:
+            meanwhile()
+        each(n_xy, lambda d: landed(recv1, 0, xy_peer(d), mid.at[t, take]))
+        value = recv1[t, 0, :nm]
+        for i in range(1, n_xy):
+            value = value + recv1[t, i, :nm]
+        mid[t, :nm] = value
+        each(n_zc, lambda d: second(d).start())
+        recv2[t, zc, :nm] = value
+        each(n_zc, lambda d: landed(recv2, 1, zc_peer(d), mid.at[t, take]))
+        value = recv2[t, 0, :nm]
+        for i in range(1, n_zc):
+            value = value + recv2[t, i, :nm]
+        fin[t, :nm] = value
+        each(n_xy, lambda d: third(d).start())
+        total[t, xy, :nm] = value
+        each(n_xy, lambda d: landed(total, 2, xy_peer(d), fin.at[t, take]))
+        each(n_xy, lambda d: first(d).wait_send())
+        each(n_zc, lambda d: second(d).wait_send())
+        each(n_xy, lambda d: third(d).wait_send())
+        return [total[t, :, m].reshape(width, width) for m in range(nm)]
+
+    def factor(matrix, beside):
+        work[:, :width] = matrix
+        eye = lax.broadcasted_iota(jnp.int32, (width, width), 0) == lax.broadcasted_iota(
+            jnp.int32, (width, width), 1
+        )
+        work[:, width:] = jnp.where(eye, 1.0, 0.0).astype(F32)
+        row = lax.broadcasted_iota(jnp.int32, (8, width), 0)
+        lane = lax.broadcasted_iota(jnp.int32, (8, width), 1)
+
+        def panel(p, carry):
+            k0 = pl.multiple_of(p * 8, 8)
+            own = pltpu.roll(work[pl.ds(k0, 8), :width], lax.rem(width - k0, width), 1)
+            right = work[pl.ds(k0, 8), width:]
+            beside(p)
+            for j in range(8):
+                column = jnp.broadcast_to(own[:, j : j + 1], (8, width))
+                scaled = lax.rsqrt(jnp.broadcast_to(column[j : j + 1], (8, width)))
+                column = column * scaled
+                line = jnp.broadcast_to(own[j : j + 1], (8, width)) * scaled
+                own = jnp.where(row > j, own - column * line, jnp.where(row == j, line, own))
+                line = jnp.broadcast_to(right[j : j + 1], (8, width)) * scaled
+                right = jnp.where(row > j, right - column * line, jnp.where(row == j, line, right))
+            upper = jnp.where(lane >= k0 + row, pltpu.roll(own, k0, 1), 0.0)
+            fac[pl.ds(k0, 8), :] = upper
+            inv[pl.ds(k0, 8), :] = right
+            both_parts = jnp.concatenate([upper, right], axis=1)
+            later = jnp.where(lane >= k0 + 8, upper, 0.0)
+            b1 = both_parts.astype(BF16).astype(F32)
+            b2 = (both_parts - b1).astype(BF16).astype(F32)
+            b3 = both_parts - b1 - b2
+            a1 = later.astype(BF16).astype(F32)
+            a2 = (later - a1).astype(BF16).astype(F32)
+            a3 = later - a1 - a2
+            left = jnp.concatenate([a1, a1, a2, a2, a1, a3], axis=0).astype(BF16)
+            rights = jnp.concatenate([b1, b2, b1, b2, b3, b1], axis=0).astype(BF16)
+            work[...] = work[...] - dot_rows(left, rights)
+            return carry
+
+        lax.fori_loop(0, width // 8, panel, 0)
+        diag = jnp.sum(jnp.where(eye, carry_gram[0], 0.0), axis=0, keepdims=True)
+        inverse = inv[...]
+        cond[...] = cond[...] + diag * jnp.sum(inverse * inverse, axis=0, keepdims=True)
+        lb[...] = square(inverse.T)
+
+    carry_gram = [None]
+
+    def form_basis(t):
+        def body(i, carry):
+            here = pl.ds(pl.multiple_of(i * bs, bs), bs)
+            q = halves(dot(both(mf[here, :]), lb[...]))
+            qf[t, here, :] = q
+            if t < STEPS:
+                high, low = split2(q)
+                qs[t, here, :] = jnp.concatenate([high, low], axis=1)
+                ext[stride + W + i] = high
+            return carry
+
+        lax.fori_loop(0, nb, body, 0)
+
+    cond[...] = jnp.zeros_like(cond)
+    hess_ref[...] = jnp.zeros_like(hess_ref)
+    gram[0] = jnp.zeros_like(gram[0])
+
+    def start_part(i, carry):
+        here = pl.ds(pl.multiple_of(i * bs, bs), bs)
+        value = start_ref[here, :]
+        mf[here, :] = value
+        pair = both(value)
+        accumulate([pair], pair)
+        return carry
+
+    lax.fori_loop(0, nb, start_part, 0)
+    publish(0, 1)
+    beside_span = 3 - (s == 0).astype(jnp.int32) - (s == n_span - 1).astype(jnp.int32)
+    beside_band = 3 - (z == 0).astype(jnp.int32) - (z == n_band - 1).astype(jnp.int32)
+    pl.semaphore_wait(barrier, n_xy + n_zc - 3 + beside_span * beside_band)
+
+    def expand_diag():
+        def body(c, carry):
+            line = jnp.broadcast_to(diag_ref[pl.ds(c, 1), :], (width, width))
+            dg[pl.ds(pl.multiple_of(c * width, width), width), :] = line.T
+            return carry
+
+        lax.fori_loop(0, rows // width, body, 0)
+
+    (matrix,) = all_reduce(0, 1, expand_diag)
+    carry_gram[0] = matrix
+    factor(matrix, lambda p: None)
+    first_ref[...] = fac[...]
+    form_basis(0)
+    load.wait()
+
+    for j in range(STEPS):
+        for n, (ds, db) in enumerate(ways):
+
+            @pl.when(reaches(ds, db))
+            def _(n=n):
+                halo_copy(n).start()
+
+        for m in range(j + 2):
+            gram[m] = jnp.zeros_like(gram[m])
+        for n, (ds, db) in enumerate(ways):
+
+            @pl.when(reaches(-ds, -db))
+            def _(n=n):
+                halo_copy(n).wait_recv()
+
+        def block_row(i, carry, j=j):
+            here = pl.ds(pl.multiple_of(i * bs, bs), bs)
+            acc = dg[here, :] * qf[j, here, :]
+            for k in range(kc):
+                at = (spans_ref[i, k] + 1) * stride + i + W + cols_ref[i, k]
+                acc = acc + dot(blk[i, k], ext[at])
+            mf[here, :] = acc
+            pair = both(acc)
+            accumulate([qs[m, here, :] for m in range(j + 1)] + [pair], pair)
+            return carry
+
+        lax.fori_loop(0, nb, block_row, 0)
+        publish(j + 1, j + 2)
+        for n, (ds, db) in enumerate(ways):
+
+            @pl.when(reaches(ds, db))
+            def _(n=n):
+                halo_copy(n).wait_send()
+
+        sums = all_reduce(j + 1, j + 2)
+        matrix = sums[j + 1]
+        carry_gram[0] = matrix
+        for i in range(j + 1):
+            hess_ref[i * width : (i + 1) * width, j * width : (j + 1) * width] = sums[i]
+            hb[i] = square(sums[i])
+            matrix = matrix - dot_rows(sums[i], sums[i], HIGHEST)
+
+        def residual_part(p, j=j):
+            here = pl.ds(pl.multiple_of(p * (rows // (width // 8)), rows // (width // 8)), rows // (width // 8))
+            value = mf[here, :]
+            for i in range(j + 1):
+                value = value - halves(dot(qs[i, here, :], hb[i]))
+            mf[here, :] = value
+
+        factor(matrix, residual_part)
+        hess_ref[(j + 1) * width : (j + 2) * width, j * width : (j + 1) * width] = fac[...]
+        form_basis(j + 1)
+        pltpu.make_async_copy(qf.at[j + 1], bases_ref.at[j], out_sem.at[j]).start()
+
+    flag_ref[0, 0] = jnp.sum(cond[...])
+    for j in range(STEPS):
+        pltpu.make_async_copy(qf.at[j + 1], bases_ref.at[j], out_sem.at[j]).wait()
+
+
+def short_form(start_block, diagonal, blocks, span_offsets, col_offsets):
+    n_span, n_band = lax.axis_size("span"), lax.axis_size("band")
+    nb, kc, bs, _ = blocks.shape
+    rows, width = start_block.shape
+    dims = (n_span, n_band, nb, bs, width, kc)
+    n_xy, n_zc = n_span // 2, n_band * 2
+    stride = nb + 2 * W
+    nm = STEPS + 1
+    chunk = width // n_xy
+    vmem = pl.BlockSpec(memory_space=pltpu.VMEM)
+    smem = pl.BlockSpec(memory_space=pltpu.SMEM)
+    anywhere = pl.BlockSpec(memory_space=pl.ANY)
+
+    def body(*refs):
+        kernel(dims, *refs)
+
+    return pl.pallas_call(
+        body,
+        out_shape=(
+            jax.ShapeDtypeStruct((STEPS, rows, width), F32),
+            jax.ShapeDtypeStruct(((STEPS + 1) * width, STEPS * width), F32),
+            jax.ShapeDtypeStruct((width, width), F32),
+            jax.ShapeDtypeStruct((1, 1), F32),
+        ),
+        in_specs=[vmem, vmem, anywhere, smem, smem],
+        out_specs=(anywhere, vmem, vmem, smem),
+        scratch_shapes=[
+            pltpu.VMEM((nb, kc, bs, bs), BF16),
+            pltpu.VMEM((3 * stride, bs, width), BF16),
+            pltpu.VMEM((STEPS + 1, rows, width), F32),
+            pltpu.VMEM((STEPS, rows, 2 * width), BF16),
+            pltpu.VMEM((rows, width), F32),
+            pltpu.VMEM((rows, width), F32),
+            pltpu.VMEM((nm, 2 * width, 2 * width), F32),
+            pltpu.VMEM((width, 2 * width), F32),
+            pltpu.VMEM((width, width), F32),
+            pltpu.VMEM((width, width), F32),
+            pltpu.VMEM((STEPS, 2 * width, 2 * width), BF16),
+            pltpu.VMEM((2 * width, 2 * width), BF16),
+            pltpu.VMEM((nm, n_xy, nm, chunk, width), F32),
+            pltpu.VMEM((nm, n_xy, nm, chunk, width), F32),
+            pltpu.VMEM((nm, nm, chunk, width), F32),
+            pltpu.VMEM((nm, n_zc, nm, chunk, width), F32),
+            pltpu.VMEM((nm, nm, chunk, width), F32),
+            pltpu.VMEM((nm, n_xy, nm, chunk, width), F32),
+            pltpu.VMEM((1, width), F32),
+            pltpu.SemaphoreType.DMA((3, max(n_xy, n_zc))),
+            pltpu.SemaphoreType.DMA((2, 3, max(n_xy, n_zc))),
+            pltpu.SemaphoreType.DMA((8,)),
+            pltpu.SemaphoreType.DMA((8,)),
+            pltpu.SemaphoreType.DMA,
+            pltpu.SemaphoreType.DMA((STEPS,)),
+        ],
+        compiler_params=pltpu.CompilerParams(
+            collective_id=0, has_side_effects=True, vmem_limit_bytes=48 * 1024 * 1024
+        ),
+    )(start_block, diagonal.reshape(rows // width, width), blocks, span_offsets, col_offsets)
+
+
+def per_device(start_block, diagonal, blocks, span_offsets, col_offsets):
+    args = (start_block, diagonal, blocks, span_offsets, col_offsets)
+    bases_out, hessenberg, r_first, spread = short_form(*args)
+    return lax.cond(
+        spread[0, 0] <= LIMIT,
+        lambda: (bases_out, hessenberg, r_first),
+        lambda: plain_form(*args),
+    )
+
+
 def solution(mesh):
     placed = (
         P(("span", "band"), None),

time: 2030 us -> 240 us (0.12)
  waiting for transfers between devices: 1720 us -> 0 us
  Pallas kernels: 0 us -> 220 us
  other arithmetic: 114 us -> 0 us
  local copies, waits for them, and re-layouts: 72.9 us -> 5.36 us
  matrix products: 64.1 us -> 0 us
  starting transfers between devices: 29.6 us -> 0 us
    psum x7 -> x0, waiting for transfers between devices: 1680 us -> none  [the longest x3 727 us: per_device(): coeffs = lax.psum(partials, ('span', 'band'))]
    pallas_call x0 -> x1, Pallas kernels: none -> 220 us  [short_form(): pl.pallas_call(body, out_shape=(jax.ShapeDtypeStruct((STEPS, rows, width)...]
    another operation x19 -> x0, other arithmetic: 92.1 us -> none  [the longest x12 49.6 us: from_gram(): upper_fac = jnp.linalg.cholesky(gram_mat).T]
    dot_general x23 -> x0, matrix products: 62.9 us -> none  [the longest x3 23.5 us: apply_operator(): jnp.einsum('ikab,ikbc->iac', blocks, picked, preferred_element_type=jnp.f...]
    ppermute x12 -> x0, waiting for transfers between devices: 45.3 us -> none  [the longest x6 23.3 us: padded(): lax.ppermute(lax.slice_in_dim(block, 0, width, axis=dim), axis, backward)]
    gather x6 -> x0, local copies, waits for them, and re-layouts: 33.6 us -> none  [apply_operator(): picked = jnp.take(lookup, flat_index, axis=0)]
    ppermute x12 -> x0, starting transfers between devices: 28.5 us -> none  [the longest x6 18 us: padded(): lax.ppermute(lax.slice_in_dim(block, block.shape[dim] - width, None, axis...]
  transfers between devices with their start and end apart: 19 -> 0, of which waited for: 19 -> 0; matrix products, arithmetic and copies ran while one was open for 0% -> 0% of each run, Pallas kernels for 0% -> 0%
where the time goes in v1:
time: 240 us
  Pallas kernels  220 us (92%)
  between operations  14.6 us (6%)
  local copies, waits for them, and re-layouts  5.36 us (2%)
    pallas_call x1, Pallas kernels, short_form(): pl.pallas_call(body, out_shape=(jax.ShapeDtypeStruct((STEPS, rows, width)...  220 us
    unnamed x15, local copies, waits for them, and re-layouts  5.36 us

profile of v1, /device:TPU:1, one launch (start us, length us, event | category | flops | bytes accessed | tf_op | source)
XLA Modules:
  0.0 240.4 jit_solution(15228053270964382053)
XLA Ops:
  7.2 0.0 copy-start.1
  7.2 0.0 copy-start.11
  7.2 0.0 copy-start.13
  7.2 0.0 copy-start.14
  7.2 220.1 %shard_map.82 = (f32[3,2048,128]{2,1,0:T(8,128)}, f32[512,384]{1,0:T(8,128)}, f32[128,128]{1,0:T(8,128)}, f32[1,1]{1,0:T(1,128)}) custom-call(f32[2048,128]{1,0:T(8,128)} %refs_0_.1, f32[16,128]{1,0:T(8,128)} %bitcast.154, bf16[8,8,256,256]{3,2,1,0:T(8,128)(2,1)} %refs_2_.1, s32[8,8]{1,0:T(8,128)} %refs_3_.1, s32[8,8]{1,0:T(8,128)} %refs_4_.1), custom_call_target="tpu_custom_call" | custom-call | tf_op jit(solution)/shard_map/pallas_call | solution.py:486
  227.9 0.0 copy-done.1
  227.9 0.0 copy-done.11
  227.9 0.0 copy-done.13
  227.9 0.0 copy-done.14
  227.9 0.2 conditional.1
  228.2 0.0 copy-start.4
  228.2 0.0 copy-start.12
  228.2 3.8 %copy.107 = f32[3,2048,128]{2,1,0:T(8,128)} copy(f32[3,2048,128]{2,1,0:T(8,128)} %get-tuple-element.83) | data formatting | bytes 6291456
  232.0 0.0 copy-done.4
  232.0 0.9 copy.108
  232.9 0.0 copy-done.12
  232.9 0.6 copy.109
Async XLA Ops:
  7.2 220.7 %copy-start.1 = (f32[2048,128]{1,0:T(8,128)S(1)}, f32[2048,128]{1,0:T(8,128)}, u32[]{:S(2)}) copy-start(f32[2048,128]{1,0:T(8,128)} %refs_0_.1) | copy-start | bytes 3145732
  7.2 220.7 %copy-start.11 = (f32[2048]{0:T(1024)S(1)}, f32[2048]{0:T(1024)}, u32[]{:S(2)}) copy-start(f32[2048]{0:T(1024)} %param.13) | copy-start | bytes 24580
  7.2 220.7 %copy-start.13 = (s32[8,8]{1,0:T(8,128)S(1)}, s32[8,8]{1,0:T(8,128)}, u32[]{:S(2)}) copy-start(s32[8,8]{1,0:T(8,128)} %refs_3_.1) | copy-start | bytes 772
  7.2 220.7 %copy-start.14 = (s32[8,8]{1,0:T(8,128)S(1)}, s32[8,8]{1,0:T(8,128)}, u32[]{:S(2)}) copy-start(s32[8,8]{1,0:T(8,128)} %refs_4_.1) | copy-start | bytes 772
  228.2 3.9 %copy-start.4 = (f32[512,384]{1,0:T(8,128)S(1)}, f32[512,384]{1,0:T(8,128)}, u32[]{:S(2)}) copy-start(f32[512,384]{1,0:T(8,128)} %get-tuple-element.84) | copy-start | bytes 2359300
  228.2 4.7 %copy-start.12 = (f32[128,128]{1,0:T(8,128)S(1)}, f32[128,128]{1,0:T(8,128)}, u32[]{:S(2)}) copy-start(f32[128,128]{1,0:T(8,128)} %get-tuple-element.85) | copy-start | bytes 196612

commit v2 on v1

--- a/solution.py
+++ b/solution.py
@@ -1,3 +1,5 @@
+import math
+
 import jax
 import jax.numpy as jnp
 from jax import lax
@@ -31,6 +33,16 @@
     return (
         jnp.dot(first.T, second, precision=HIGHEST, preferred_element_type=jnp.float32) / row_total
     )
+
+
+def sum_all(value):
+    for axis in ("band", "span"):
+        count = lax.axis_size(axis)
+        bit = 1
+        while bit < count:
+            value = value + lax.ppermute(value, axis, [(i, i ^ bit) for i in range(count)])
+            bit *= 2
+    return value
 
 
 def from_upper(upper_fac, matrix):
@@ -75,16 +87,16 @@
 def plain_form(start_block, diagonal, blocks, span_offsets, col_offsets):
     row_total = float(start_block.shape[0] * lax.axis_size("span") * lax.axis_size("band"))
     vec_width = start_block.shape[1]
-    first_gram = lax.psum(local_inner(start_block, start_block, row_total), ("span", "band"))
+    first_gram = sum_all(local_inner(start_block, start_block, row_total))
     r_first, current = from_gram(first_gram, start_block)
     bases = [current]
     columns = []
     for step_id in range(STEPS):
         mapped = apply_operator(bases[-1], diagonal, blocks, span_offsets, col_offsets)
         partials = jnp.stack([local_inner(earlier, mapped, row_total) for earlier in bases])
-        coeffs = lax.psum(partials, ("span", "band"))
+        coeffs = sum_all(partials)
         residual = subtract_projections(mapped, bases, coeffs)
-        gram_mat = lax.psum(local_inner(residual, residual, row_total), ("span", "band"))
+        gram_mat = sum_all(local_inner(residual, residual, row_total))
         r_next, q_next = from_gram(gram_mat, residual)
         pieces = [coeffs.reshape(len(bases) * vec_width, vec_width), r_next]
         if STEPS - 1 - step_id > 0:
@@ -104,6 +116,10 @@
     return lax.dot_general(
         a, b, (((0,), (0,)), ((), ())), precision=precision, preferred_element_type=F32
     )
+
+
+def rounded(x):
+    return x.astype(BF16).astype(F32)
 
 
 def split2(x):
@@ -151,6 +167,7 @@
     work,
     fac,
     inv,
+    spread,
     hb,
     lb,
     part,
@@ -186,6 +203,24 @@
         peer = lax.rem(zc + d, n_zc)
         return peer, (xy * 2 + lax.rem(peer, 2), peer // 2)
 
+    side = math.isqrt(n_xy)
+    x, y = xy // side, xy % side
+
+    def hops(step, count):
+        return min(step, count - step)
+
+    def xy_far(act):
+        steps = [(dx, dy) for dx in range(side) for dy in range(side) if dx or dy]
+        for dx, dy in sorted(steps, key=lambda t: -hops(t[0], side) - hops(t[1], side)):
+            peer = lax.rem(x + dx, side) * side + lax.rem(y + dy, side)
+            act((peer, (peer * 2 + core, z)))
+
+    def zc_far(act):
+        steps = [(dz, dc) for dz in range(n_band) for dc in range(2) if dz or dc]
+        for dz, dc in sorted(steps, key=lambda t: -2 * hops(t[0], n_band) - t[1]):
+            to_z, to_core = lax.rem(z + dz, n_band), lax.rem(core + dc, 2)
+            act((to_z * 2 + to_core, (xy * 2 + to_core, to_z)))
+
     ways = [(ds, db) for db in (0, -1, 1) for ds in (-1, 0, 1) if (ds, db) != (0, 0)]
 
     def reaches(ds, db):
@@ -241,8 +276,8 @@
         take = pl.ds(0, nm)
         par = t % 2
 
-        def first(d):
-            peer, device = xy_peer(d)
+        def first(who):
+            peer, device = who
             return pltpu.make_async_remote_copy(
                 src_ref=part.at[t, peer, take],
                 dst_ref=recv1.at[t, xy, take],
@@ -252,8 +287,8 @@
                 device_id_type=MESH,
             )
 
-        def second(d):
-            peer, device = zc_peer(d)
+        def second(who):
+            peer, device = who
             return pltpu.make_async_remote_copy(
                 src_ref=mid.at[t, take],
                 dst_ref=recv2.at[t, zc, take],
@@ -263,8 +298,8 @@
                 device_id_type=MESH,
             )
 
-        def third(d):
-            peer, device = xy_peer(d)
+        def third(who):
+            peer, device = who
             return pltpu.make_async_remote_copy(
                 src_ref=fin.at[t, take],
                 dst_ref=total.at[t, xy, take],
@@ -292,7 +327,7 @@
 
             lax.fori_loop(1, n, body, 0)
 
-        each(n_xy, lambda d: first(d).start())
+        xy_far(lambda who: first(who).start())
         recv1[t, xy, :nm] = part[t, xy, :nm]
         if meanwhile is not None:
             meanwhile()
@@ -301,64 +336,100 @@
         for i in range(1, n_xy):
             value = value + recv1[t, i, :nm]
         mid[t, :nm] = value
-        each(n_zc, lambda d: second(d).start())
+        zc_far(lambda who: second(who).start())
         recv2[t, zc, :nm] = value
         each(n_zc, lambda d: landed(recv2, 1, zc_peer(d), mid.at[t, take]))
         value = recv2[t, 0, :nm]
         for i in range(1, n_zc):
             value = value + recv2[t, i, :nm]
         fin[t, :nm] = value
-        each(n_xy, lambda d: third(d).start())
+        xy_far(lambda who: third(who).start())
         total[t, xy, :nm] = value
         each(n_xy, lambda d: landed(total, 2, xy_peer(d), fin.at[t, take]))
-        each(n_xy, lambda d: first(d).wait_send())
-        each(n_zc, lambda d: second(d).wait_send())
-        each(n_xy, lambda d: third(d).wait_send())
-        return [total[t, :, m].reshape(width, width) for m in range(nm)]
+
+        def sent():
+            each(n_xy, lambda d: first(xy_peer(d)).wait_send())
+            each(n_zc, lambda d: second(zc_peer(d)).wait_send())
+            each(n_xy, lambda d: third(xy_peer(d)).wait_send())
+
+        return [total[t, :, m].reshape(width, width) for m in range(nm)], sent
 
     def factor(matrix, beside):
-        work[:, :width] = matrix
-        eye = lax.broadcasted_iota(jnp.int32, (width, width), 0) == lax.broadcasted_iota(
-            jnp.int32, (width, width), 1
+        w = width
+        tile = (8, w)
+        work[:, :w] = matrix
+        eye = lax.broadcasted_iota(jnp.int32, (w, w), 0) == lax.broadcasted_iota(
+            jnp.int32, (w, w), 1
         )
-        work[:, width:] = jnp.where(eye, 1.0, 0.0).astype(F32)
-        row = lax.broadcasted_iota(jnp.int32, (8, width), 0)
-        lane = lax.broadcasted_iota(jnp.int32, (8, width), 1)
+        work[:, w:] = jnp.where(eye, 1.0, 0.0).astype(F32)
+        row = lax.broadcasted_iota(jnp.int32, tile, 0)
+        lane = lax.broadcasted_iota(jnp.int32, tile, 1)
+        lanes = lax.broadcasted_iota(jnp.int32, (w, w), 1)
+        within, group = lax.rem(lanes, 8), lanes // 8
+        firsts = (group == 0) | (group == 1) | (group == 4)
+        seconds = (group == 2) | (group == 3)
+        thirds = group == 5
+
+        def assemble(lines):
+            out = lines[7]
+            for j in range(6, -1, -1):
+                out = jnp.where(row == j, lines[j], out)
+            return out
 
         def panel(p, carry):
             k0 = pl.multiple_of(p * 8, 8)
-            own = pltpu.roll(work[pl.ds(k0, 8), :width], lax.rem(width - k0, width), 1)
-            right = work[pl.ds(k0, 8), width:]
+            pivot = work[pl.ds(k0, 8), :w]
+            for j in range(8):
+                spread[j] = jnp.take_along_axis(pivot, jnp.broadcast_to(k0 + j, tile), axis=1)
+            spread[8] = pivot
+            spread[9] = work[pl.ds(k0, 8), w:]
+            columns = jnp.take_along_axis(work[:, :w], k0 + within, axis=1)
+            a1 = rounded(columns)
+            a2 = rounded(columns - a1)
+            a3 = columns - a1 - a2
+            left = jnp.where(firsts, a1, jnp.where(seconds, a2, jnp.where(thirds, a3, 0.0)))
+            left = left.astype(BF16)[:, :48]
+
+            def line(n, i):
+                return jnp.broadcast_to(spread[n, pl.ds(i, 1), :], tile)
+
+            a = [[line(j, i) if i >= j else None for j in range(8)] for i in range(8)]
+            heads = [line(8, i) for i in range(8)]
+            tails = [line(9, i) for i in range(8)]
             beside(p)
+            by = [None] * 8
             for j in range(8):
-                column = jnp.broadcast_to(own[:, j : j + 1], (8, width))
-                scaled = lax.rsqrt(jnp.broadcast_to(column[j : j + 1], (8, width)))
-                column = column * scaled
-                line = jnp.broadcast_to(own[j : j + 1], (8, width)) * scaled
-                own = jnp.where(row > j, own - column * line, jnp.where(row == j, line, own))
-                line = jnp.broadcast_to(right[j : j + 1], (8, width)) * scaled
-                right = jnp.where(row > j, right - column * line, jnp.where(row == j, line, right))
-            upper = jnp.where(lane >= k0 + row, pltpu.roll(own, k0, 1), 0.0)
-            fac[pl.ds(k0, 8), :] = upper
-            inv[pl.ds(k0, 8), :] = right
-            both_parts = jnp.concatenate([upper, right], axis=1)
-            later = jnp.where(lane >= k0 + 8, upper, 0.0)
-            b1 = both_parts.astype(BF16).astype(F32)
-            b2 = (both_parts - b1).astype(BF16).astype(F32)
-            b3 = both_parts - b1 - b2
-            a1 = later.astype(BF16).astype(F32)
-            a2 = (later - a1).astype(BF16).astype(F32)
-            a3 = later - a1 - a2
-            left = jnp.concatenate([a1, a1, a2, a2, a1, a3], axis=0).astype(BF16)
+                by[j] = lax.rsqrt(a[j][j])
+                heads[j] = heads[j] * by[j]
+                tails[j] = tails[j] * by[j]
+                for i in range(j + 1, 8):
+                    a[i][j] = a[i][j] * by[j]
+                for i in range(j + 1, 8):
+                    for m in range(j + 1, i + 1):
+                        a[i][m] = a[i][m] - a[i][j] * a[m][j]
+                    heads[i] = heads[i] - a[i][j] * heads[j]
+                    tails[i] = tails[i] - a[i][j] * tails[j]
+            fac[pl.ds(k0, 8), :] = jnp.where(lane >= k0 + row, assemble(heads), 0.0)
+            inv[pl.ds(k0, 8), :] = assemble(tails)
+            for j in range(7, -1, -1):
+                heads[j] = heads[j] * by[j]
+                tails[j] = tails[j] * by[j]
+                for i in range(j):
+                    heads[i] = heads[i] - a[j][i] * heads[j]
+                    tails[i] = tails[i] - a[j][i] * tails[j]
+            right = jnp.concatenate([assemble(heads), assemble(tails)], axis=1)
+            b1 = rounded(right)
+            b2 = rounded(right - b1)
+            b3 = right - b1 - b2
             rights = jnp.concatenate([b1, b2, b1, b2, b3, b1], axis=0).astype(BF16)
-            work[...] = work[...] - dot_rows(left, rights)
+            work[...] = work[...] - dot(left, rights)
             return carry
 
-        lax.fori_loop(0, width // 8, panel, 0)
+        lax.fori_loop(0, w // 8, panel, 0)
+        inverse = inv[...]
+        lb[...] = square(inverse.T)
         diag = jnp.sum(jnp.where(eye, carry_gram[0], 0.0), axis=0, keepdims=True)
-        inverse = inv[...]
         cond[...] = cond[...] + diag * jnp.sum(inverse * inverse, axis=0, keepdims=True)
-        lb[...] = square(inverse.T)
 
     carry_gram = [None]
 
@@ -401,7 +472,7 @@
 
         lax.fori_loop(0, rows // width, body, 0)
 
-    (matrix,) = all_reduce(0, 1, expand_diag)
+    (matrix,), sent = all_reduce(0, 1, expand_diag)
     carry_gram[0] = matrix
     factor(matrix, lambda p: None)
     first_ref[...] = fac[...]
@@ -415,6 +486,7 @@
             def _(n=n):
                 halo_copy(n).start()
 
+        sent()
         for m in range(j + 2):
             gram[m] = jnp.zeros_like(gram[m])
         for n, (ds, db) in enumerate(ways):
@@ -436,13 +508,14 @@
 
         lax.fori_loop(0, nb, block_row, 0)
         publish(j + 1, j + 2)
-        for n, (ds, db) in enumerate(ways):
-
-            @pl.when(reaches(ds, db))
-            def _(n=n):
-                halo_copy(n).wait_send()
-
-        sums = all_reduce(j + 1, j + 2)
+        def halo_sent():
+            for n, (ds, db) in enumerate(ways):
+
+                @pl.when(reaches(ds, db))
+                def _(n=n):
+                    halo_copy(n).wait_send()
+
+        sums, sent = all_reduce(j + 1, j + 2, halo_sent)
         matrix = sums[j + 1]
         carry_gram[0] = matrix
         for i in range(j + 1):
@@ -462,6 +535,7 @@
         form_basis(j + 1)
         pltpu.make_async_copy(qf.at[j + 1], bases_ref.at[j], out_sem.at[j]).start()
 
+    sent()
     flag_ref[0, 0] = jnp.sum(cond[...])
     for j in range(STEPS):
         pltpu.make_async_copy(qf.at[j + 1], bases_ref.at[j], out_sem.at[j]).wait()
@@ -504,6 +578,7 @@
             pltpu.VMEM((width, 2 * width), F32),
             pltpu.VMEM((width, width), F32),
             pltpu.VMEM((width, width), F32),
+            pltpu.VMEM((10, 8, width), F32),
             pltpu.VMEM((STEPS, 2 * width, 2 * width), BF16),
             pltpu.VMEM((2 * width, 2 * width), BF16),
             pltpu.VMEM((nm, n_xy, nm, chunk, width), F32),
@@ -526,12 +601,37 @@
     )(start_block, diagonal.reshape(rows // width, width), blocks, span_offsets, col_offsets)
 
 
+def hand_over(bases_out, hessenberg, r_first):
+    parts = bases_out.shape[0]
+
+    def body(bases, hess, first, bases_to, hess_to, first_to, sems):
+        copies = [
+            pltpu.make_async_copy(bases.at[i], bases_to.at[i], sems.at[i]) for i in range(parts)
+        ]
+        copies.append(pltpu.make_async_copy(hess, hess_to, sems.at[parts]))
+        copies.append(pltpu.make_async_copy(first, first_to, sems.at[parts + 1]))
+        for copy in copies:
+            copy.start()
+        for copy in copies:
+            copy.wait()
+
+    arrays = (bases_out, hessenberg, r_first)
+    anywhere = pl.BlockSpec(memory_space=pl.ANY)
+    return pl.pallas_call(
+        body,
+        out_shape=tuple(jax.ShapeDtypeStruct(a.shape, a.dtype) for a in arrays),
+        in_specs=[anywhere] * 3,
+        out_specs=(anywhere,) * 3,
+        scratch_shapes=[pltpu.SemaphoreType.DMA((parts + 2,))],
+    )(*arrays)
+
+
 def per_device(start_block, diagonal, blocks, span_offsets, col_offsets):
     args = (start_block, diagonal, blocks, span_offsets, col_offsets)
     bases_out, hessenberg, r_first, spread = short_form(*args)
     return lax.cond(
         spread[0, 0] <= LIMIT,
-        lambda: (bases_out, hessenberg, r_first),
+        lambda: hand_over(bases_out, hessenberg, r_first),
         lambda: plain_form(*args),
     )
 

time: 240 us -> 281 us (1.17)
  Pallas kernels: 220 us -> 279 us
  between operations: 14.6 us -> 1.5 us
  local copies, waits for them, and re-layouts: 5.36 us -> 0.02 us
    pallas_call x0 -> x1, Pallas kernels: none -> 122 us  [hand_over(): pl.pallas_call(body, out_shape=tuple((jax.ShapeDtypeStruct(a.shape, a.dty...]
    pallas_call x1, Pallas kernels: 220 us -> 157 us  [short_form(): pl.pallas_call(body, out_shape=(jax.ShapeDtypeStruct((STEPS, rows, width)...]
    unnamed x15 -> x8, local copies, waits for them, and re-layouts: 5.36 us -> 0.02 us
where the time goes in v2:
time: 281 us
  Pallas kernels  279 us (99%)
    pallas_call x1, Pallas kernels, short_form(): pl.pallas_call(body, out_shape=(jax.ShapeDtypeStruct((STEPS, rows, width)...  157 us
    pallas_call x1, Pallas kernels, hand_over(): pl.pallas_call(body, out_shape=tuple((jax.ShapeDtypeStruct(a.shape, a.dty...  122 us

profile of v2, /device:TPU:1, one launch (start us, length us, event | category | flops | bytes accessed | tf_op | source)
XLA Modules:
  0.0 280.7 jit_solution(9685483116264841006)
XLA Ops:
  0.6 0.0 copy-start
  0.6 0.0 copy-start.9
  0.7 0.0 copy-start.10
  0.7 0.0 copy-start.11
  0.7 156.7 %shard_map.82 = (f32[3,2048,128]{2,1,0:T(8,128)}, f32[512,384]{1,0:T(8,128)}, f32[128,128]{1,0:T(8,128)}, f32[1,1]{1,0:T(1,128)}) custom-call(f32[2048,128]{1,0:T(8,128)} %refs_0_.1, f32[16,128]{1,0:T(8,128)} %bitcast.158, bf16[8,8,256,256]{3,2,1,0:T(8,128)(2,1)} %refs_2_.1, s32[8,8]{1,0:T(8,128)} %refs_3_.1, s32[8,8]{1,0:T(8,128)} %refs_4_.1), custom_call_target="tpu_custom_call" | custom-call | tf_op jit(solution)/shard_map/pallas_call | solution.py:560
  158.0 0.0 copy-done
  158.0 0.0 copy-done.9
  158.0 0.0 copy-done.10
  158.0 0.0 copy-done.11
  158.0 122.5 %conditional.1 = ((f32[3,2048,128]{2,1,0:T(8,128)}, f32[512,384]{1,0:T(8,128)}, f32[128,128]{1,0:T(8,128)})) conditional(s32[]{:T(128)} %bitcast.50, (f32[2048]{0:T(1024)S(1)}, f32[2048,128]{1,0:T(8,128)S(1)}, s32[8,8]{1,0:T(8,128)S(1)}, s32[8,8]{1,0:T(8,128)S(1)}, bf16[8,8,256,256]{3,2,1,0:T(8,128)(2,1)}) %tuple.48, (f32[3,2048,128]{2,1,0:T(8,128)}, ...), branch_computations={%region_0.0_spmd, %region_3.7_spmd} | conditional | flops 11412555776 | bytes 290633440 | solution.py:632
  158.2 122.2 %branch_1_fun.1 = (f32[3,2048,128]{2,1,0:T(8,128)}, f32[512,384]{1,0:T(8,128)}, f32[128,128]{1,0:T(8,128)}) custom-call(f32[3,2048,128]{2,1,0:T(8,128)} %get-tuple-element.24.bases, f32[512,384]{1,0:T(8,128)} %get-tuple-element.25.hess, f32[128,128]{1,0:T(8,128)} %get-tuple-element.26.first), custom_call_target="tpu_custom_call" | custom-call | tf_op jit(solution)/shard_map/cond/branch_1_fun/pallas_call | solution.py:620
Async XLA Ops:
  0.6 157.3 %copy-start = (f32[2048,128]{1,0:T(8,128)S(1)}, f32[2048,128]{1,0:T(8,128)}, u32[]{:S(2)}) copy-start(f32[2048,128]{1,0:T(8,128)} %refs_0_.1) | copy-start | bytes 3145732
  0.6 157.3 %copy-start.9 = (f32[2048]{0:T(1024)S(1)}, f32[2048]{0:T(1024)}, u32[]{:S(2)}) copy-start(f32[2048]{0:T(1024)} %param.13) | copy-start | bytes 24580
  0.7 157.3 %copy-start.10 = (s32[8,8]{1,0:T(8,128)S(1)}, s32[8,8]{1,0:T(8,128)}, u32[]{:S(2)}) copy-start(s32[8,8]{1,0:T(8,128)} %refs_3_.1) | copy-start | bytes 772
  0.7 157.3 %copy-start.11 = (s32[8,8]{1,0:T(8,128)S(1)}, s32[8,8]{1,0:T(8,128)}, u32[]{:S(2)}) copy-start(s32[8,8]{1,0:T(8,128)} %refs_4_.1) | copy-start | bytes 772

commit v3 on v2

--- a/solution.py
+++ b/solution.py
@@ -154,6 +154,8 @@
     spans_ref,
     cols_ref,
     bases_ref,
+    rest_ref,
+    inverse_ref,
     hess_ref,
     first_ref,
     flag_ref,
@@ -221,32 +223,85 @@
             to_z, to_core = lax.rem(z + dz, n_band), lax.rem(core + dc, 2)
             act((to_z * 2 + to_core, (xy * 2 + to_core, to_z)))
 
-    ways = [(ds, db) for db in (0, -1, 1) for ds in (-1, 0, 1) if (ds, db) != (0, 0)]
-
-    def reaches(ds, db):
-        return (s + ds >= 0) & (s + ds < n_span) & (z + db >= 0) & (z + db < n_band)
-
-    def halo_copy(n):
-        ds, db = ways[n]
-        seg = (1 - ds) * stride
-        if db == 0:
-            source, target, count = W, W, nb
-        elif db == 1:
-            source, target, count = nb, 0, W
-        else:
-            source, target, count = W, nb + W, W
+    sibling, beyond = s + 1 - 2 * core, s - 1 + 2 * core
+    has_beyond = (beyond >= 0) & (beyond < n_span)
+    has_below, has_above = z > 0, z < n_band - 1
+    near_seg, far_seg = (2 - 2 * core) * stride, 2 * core * stride
+    always = z >= 0
+    low, high = W, nb
+    top = nb + W
+
+    moves = [
+        (stride + low, near_seg + low, W, (beyond, z), has_beyond, far_seg + low, has_beyond),
+        (stride + high, near_seg + high, W, (beyond, z), has_beyond, far_seg + high, has_beyond),
+        (stride + low, stride + top, W, (s, z - 1), has_below, stride + top, has_above),
+        (stride + high, stride, W, (s, z + 1), has_above, stride, has_below),
+        (stride + low, far_seg + low, nb, (sibling, z), always, near_seg + low, always),
+        (
+            stride + low + W,
+            near_seg + low + W,
+            nb - 2 * W,
+            (beyond, z),
+            has_beyond,
+            far_seg + low + W,
+            has_beyond,
+        ),
+        (stride, far_seg, W, (sibling, z), has_below, near_seg, has_below),
+        (stride + top, far_seg + top, W, (sibling, z), has_above, near_seg + top, has_above),
+        (
+            far_seg + high,
+            far_seg,
+            W,
+            (s, z + 1),
+            has_beyond & has_above,
+            far_seg,
+            has_beyond & has_below,
+        ),
+        (
+            far_seg + low,
+            far_seg + top,
+            W,
+            (s, z - 1),
+            has_beyond & has_below,
+            far_seg + top,
+            has_beyond & has_above,
+        ),
+    ]
+
+    def move(n, source, target, count, device):
         return pltpu.make_async_remote_copy(
-            src_ref=ext.at[pl.ds(stride + source, count)],
-            dst_ref=ext.at[pl.ds(seg + target, count)],
+            src_ref=ext.at[pl.ds(source, count)],
+            dst_ref=ext.at[pl.ds(target, count)],
             send_sem=halo_send.at[n],
             recv_sem=halo_recv.at[n],
-            device_id=(s + ds, z + db),
+            device_id=device,
             device_id_type=MESH,
         )
 
-    load = pltpu.make_async_copy(blocks_ref, blk, blk_sem)
-    load.start()
-    ext[...] = jnp.zeros_like(ext)
+    def send(*chosen):
+        for n in chosen:
+            source, target, count, device, goes, _, _ = moves[n]
+
+            @pl.when(goes)
+            def _():
+                move(n, source, target, count, device).start()
+
+    def sent_halo(*chosen):
+        for n in chosen:
+            source, target, count, device, goes, _, _ = moves[n]
+
+            @pl.when(goes)
+            def _():
+                move(n, source, target, count, device).wait_send()
+
+    def arrived(*chosen):
+        for n in chosen:
+            source, _, count, device, _, here, comes = moves[n]
+
+            @pl.when(comes)
+            def _():
+                move(n, source, here, count, device).wait_recv()
+
     barrier = pltpu.get_barrier_semaphore()
 
     def greet(peer_of):
@@ -258,11 +313,13 @@
 
     lax.fori_loop(1, n_xy, greet(xy_peer), 0)
     lax.fori_loop(1, n_zc, greet(zc_peer), 0)
-    for ds, db in ways:
-
-        @pl.when(reaches(ds, db))
-        def _():
-            pl.semaphore_signal(barrier, inc=1, device_id=(s + ds, z + db), device_id_type=MESH)
+
+    @pl.when(has_beyond)
+    def _():
+        pl.semaphore_signal(barrier, inc=1, device_id=(beyond, z), device_id_type=MESH)
+
+    load = pltpu.make_async_copy(blocks_ref, blk, blk_sem)
+    load.start()
 
     def accumulate(lefts, right):
         for m, left in enumerate(lefts):
@@ -434,17 +491,26 @@
     carry_gram = [None]
 
     def form_basis(t):
-        def body(i, carry):
+        def form(i):
             here = pl.ds(pl.multiple_of(i * bs, bs), bs)
             q = halves(dot(both(mf[here, :]), lb[...]))
             qf[t, here, :] = q
-            if t < STEPS:
-                high, low = split2(q)
-                qs[t, here, :] = jnp.concatenate([high, low], axis=1)
-                ext[stride + W + i] = high
+            high, low = split2(q)
+            qs[t, here, :] = jnp.concatenate([high, low], axis=1)
+            ext[stride + W + i] = high
+
+        def ends(e, carry):
+            form(jnp.where(e < W, e, e + nb - 2 * W))
             return carry
 
-        lax.fori_loop(0, nb, body, 0)
+        def middle(i, carry):
+            form(i)
+            return carry
+
+        lax.fori_loop(0, 2 * W, ends, 0)
+        send(0, 1, 2, 3)
+        lax.fori_loop(W, nb - W, middle, 0)
+        send(4, 5)
 
     cond[...] = jnp.zeros_like(cond)
     hess_ref[...] = jnp.zeros_like(hess_ref)
@@ -460,11 +526,11 @@
 
     lax.fori_loop(0, nb, start_part, 0)
     publish(0, 1)
-    beside_span = 3 - (s == 0).astype(jnp.int32) - (s == n_span - 1).astype(jnp.int32)
-    beside_band = 3 - (z == 0).astype(jnp.int32) - (z == n_band - 1).astype(jnp.int32)
-    pl.semaphore_wait(barrier, n_xy + n_zc - 3 + beside_span * beside_band)
+    pl.semaphore_wait(barrier, n_xy + n_zc - 2 + has_beyond.astype(jnp.int32))
 
     def expand_diag():
+        ext[...] = jnp.zeros_like(ext)
+
         def body(c, carry):
             line = jnp.broadcast_to(diag_ref[pl.ds(c, 1), :], (width, width))
             dg[pl.ds(pl.multiple_of(c * width, width), width), :] = line.T
@@ -476,24 +542,24 @@
     carry_gram[0] = matrix
     factor(matrix, lambda p: None)
     first_ref[...] = fac[...]
-    form_basis(0)
     load.wait()
 
     for j in range(STEPS):
-        for n, (ds, db) in enumerate(ways):
-
-            @pl.when(reaches(ds, db))
-            def _(n=n):
-                halo_copy(n).start()
-
+        form_basis(j)
+        if j > 0:
+            pltpu.make_async_copy(qf.at[j], bases_ref.at[j - 1], out_sem.at[j - 1]).start()
         sent()
         for m in range(j + 2):
             gram[m] = jnp.zeros_like(gram[m])
-        for n, (ds, db) in enumerate(ways):
-
-            @pl.when(reaches(-ds, -db))
-            def _(n=n):
-                halo_copy(n).wait_recv()
+        arrived(3)
+        send(6)
+        arrived(2)
+        send(7)
+        arrived(1)
+        send(8)
+        arrived(0)
+        send(9)
+        arrived(4, 5, 6, 7, 8, 9)
 
         def block_row(i, carry, j=j):
             here = pl.ds(pl.multiple_of(i * bs, bs), bs)
@@ -507,15 +573,9 @@
             return carry
 
         lax.fori_loop(0, nb, block_row, 0)
+        sent_halo(6, 7, 8, 9)
         publish(j + 1, j + 2)
-        def halo_sent():
-            for n, (ds, db) in enumerate(ways):
-
-                @pl.when(reaches(ds, db))
-                def _(n=n):
-                    halo_copy(n).wait_send()
-
-        sums, sent = all_reduce(j + 1, j + 2, halo_sent)
+        sums, sent = all_reduce(j + 1, j + 2, lambda: sent_halo(0, 1, 2, 3, 4, 5))
         matrix = sums[j + 1]
         carry_gram[0] = matrix
         for i in range(j + 1):
@@ -532,13 +592,15 @@
 
         factor(matrix, residual_part)
         hess_ref[(j + 1) * width : (j + 2) * width, j * width : (j + 1) * width] = fac[...]
-        form_basis(j + 1)
-        pltpu.make_async_copy(qf.at[j + 1], bases_ref.at[j], out_sem.at[j]).start()
-
+
+    last = pltpu.make_async_copy(mf, rest_ref, out_sem.at[STEPS - 1])
+    last.start()
     sent()
+    inverse_ref[...] = lb[...]
     flag_ref[0, 0] = jnp.sum(cond[...])
-    for j in range(STEPS):
-        pltpu.make_async_copy(qf.at[j + 1], bases_ref.at[j], out_sem.at[j]).wait()
+    for j in range(1, STEPS):
+        pltpu.make_async_copy(qf.at[j], bases_ref.at[j - 1], out_sem.at[j - 1]).wait()
+    last.wait()
 
 
 def short_form(start_block, diagonal, blocks, span_offsets, col_offsets):
@@ -560,17 +622,19 @@
     return pl.pallas_call(
         body,
         out_shape=(
-            jax.ShapeDtypeStruct((STEPS, rows, width), F32),
+            jax.ShapeDtypeStruct((STEPS - 1, rows, width), F32),
+            jax.ShapeDtypeStruct((rows, width), F32),
+            jax.ShapeDtypeStruct((2 * width, 2 * width), BF16),
             jax.ShapeDtypeStruct(((STEPS + 1) * width, STEPS * width), F32),
             jax.ShapeDtypeStruct((width, width), F32),
             jax.ShapeDtypeStruct((1, 1), F32),
         ),
         in_specs=[vmem, vmem, anywhere, smem, smem],
-        out_specs=(anywhere, vmem, vmem, smem),
+        out_specs=(anywhere, anywhere, vmem, vmem, vmem, smem),
         scratch_shapes=[
             pltpu.VMEM((nb, kc, bs, bs), BF16),
             pltpu.VMEM((3 * stride, bs, width), BF16),
-            pltpu.VMEM((STEPS + 1, rows, width), F32),
+            pltpu.VMEM((STEPS, rows, width), F32),
             pltpu.VMEM((STEPS, rows, 2 * width), BF16),
             pltpu.VMEM((rows, width), F32),
             pltpu.VMEM((rows, width), F32),
@@ -590,8 +654,8 @@
             pltpu.VMEM((1, width), F32),
             pltpu.SemaphoreType.DMA((3, max(n_xy, n_zc))),
             pltpu.SemaphoreType.DMA((2, 3, max(n_xy, n_zc))),
-            pltpu.SemaphoreType.DMA((8,)),
-            pltpu.SemaphoreType.DMA((8,)),
+            pltpu.SemaphoreType.DMA((10,)),
+            pltpu.SemaphoreType.DMA((10,)),
             pltpu.SemaphoreType.DMA,
             pltpu.SemaphoreType.DMA((STEPS,)),
         ],
@@ -601,37 +665,72 @@
     )(start_block, diagonal.reshape(rows // width, width), blocks, span_offsets, col_offsets)
 
 
-def hand_over(bases_out, hessenberg, r_first):
-    parts = bases_out.shape[0]
-
-    def body(bases, hess, first, bases_to, hess_to, first_to, sems):
-        copies = [
-            pltpu.make_async_copy(bases.at[i], bases_to.at[i], sems.at[i]) for i in range(parts)
+def finish(bases, rest, inverse, hessenberg, r_first):
+    before, rows, width = bases.shape
+    chunks = 4
+    chunk = rows // chunks
+
+    def body(
+        bases_ref, rest_ref, inverse_ref, hess_ref, first_ref, bases_to, hess_to, first_to, *scratch
+    ):
+        q, r, out, hess, first, in_sem, out_sem = scratch
+        parts = [pl.ds(i * chunk, chunk) for i in range(chunks)]
+        loads = [
+            pltpu.make_async_copy(rest_ref.at[here], r.at[here], in_sem.at[i])
+            for i, here in enumerate(parts)
         ]
-        copies.append(pltpu.make_async_copy(hess, hess_to, sems.at[parts]))
-        copies.append(pltpu.make_async_copy(first, first_to, sems.at[parts + 1]))
-        for copy in copies:
-            copy.start()
-        for copy in copies:
-            copy.wait()
-
-    arrays = (bases_out, hessenberg, r_first)
+        others = [(bases_ref.at[i], q.at[i], bases_to.at[i]) for i in range(before)]
+        others += [(hess_ref, hess, hess_to), (first_ref, first, first_to)]
+        for i, (source, held, _) in enumerate(others):
+            loads.append(pltpu.make_async_copy(source, held, in_sem.at[chunks + i]))
+        for load in loads:
+            load.start()
+        stores = []
+        for i, here in enumerate(parts):
+            loads[i].wait()
+            out[here, :] = halves(dot(both(r[here, :]), inverse_ref[...]))
+            stores.append(
+                pltpu.make_async_copy(out.at[here], bases_to.at[before, here], out_sem.at[i])
+            )
+            stores[-1].start()
+            if i < len(others):
+                loads[chunks + i].wait()
+                _, held, target = others[i]
+                stores.append(pltpu.make_async_copy(held, target, out_sem.at[chunks + i]))
+                stores[-1].start()
+        for store in stores:
+            store.wait()
+
     anywhere = pl.BlockSpec(memory_space=pl.ANY)
+    vmem = pl.BlockSpec(memory_space=pltpu.VMEM)
     return pl.pallas_call(
         body,
-        out_shape=tuple(jax.ShapeDtypeStruct(a.shape, a.dtype) for a in arrays),
-        in_specs=[anywhere] * 3,
+        out_shape=(
+            jax.ShapeDtypeStruct((before + 1, rows, width), F32),
+            jax.ShapeDtypeStruct(hessenberg.shape, F32),
+            jax.ShapeDtypeStruct(r_first.shape, F32),
+        ),
+        in_specs=[anywhere, anywhere, vmem, anywhere, anywhere],
         out_specs=(anywhere,) * 3,
-        scratch_shapes=[pltpu.SemaphoreType.DMA((parts + 2,))],
-    )(*arrays)
+        scratch_shapes=[
+            pltpu.VMEM(bases.shape, F32),
+            pltpu.VMEM((rows, width), F32),
+            pltpu.VMEM((rows, width), F32),
+            pltpu.VMEM(hessenberg.shape, F32),
+            pltpu.VMEM(r_first.shape, F32),
+            pltpu.SemaphoreType.DMA((chunks + before + 2,)),
+            pltpu.SemaphoreType.DMA((chunks + before + 2,)),
+        ],
+        compiler_params=pltpu.CompilerParams(vmem_limit_bytes=16 * 1024 * 1024),
+    )(bases, rest, inverse, hessenberg, r_first)
 
 
 def per_device(start_block, diagonal, blocks, span_offsets, col_offsets):
     args = (start_block, diagonal, blocks, span_offsets, col_offsets)
-    bases_out, hessenberg, r_first, spread = short_form(*args)
+    *parts, spread = short_form(*args)
     return lax.cond(
         spread[0, 0] <= LIMIT,
-        lambda: hand_over(bases_out, hessenberg, r_first),
+        lambda: finish(*parts),
         lambda: plain_form(*args),
     )
 

time: 281 us -> 156 us (0.56)
  Pallas kernels: 279 us -> 154 us
    pallas_call x2, Pallas kernels: 279 us -> 154 us  [the longest x1 150 us: short_form(): pl.pallas_call(body, out_shape=(jax.ShapeDtypeStruct((STEPS - 1, rows, wi...]
where the time goes in v3:
time: 156 us
  Pallas kernels  154 us (99%)
    pallas_call x1, Pallas kernels, short_form(): pl.pallas_call(body, out_shape=(jax.ShapeDtypeStruct((STEPS - 1, rows, wi...  150 us
    pallas_call x1, Pallas kernels, finish(): pl.pallas_call(body, out_shape=(jax.ShapeDtypeStruct((before + 1, rows, w...  4.43 us

profile of v3, /device:TPU:1, one launch (start us, length us, event | category | flops | bytes accessed | tf_op | source)
XLA Modules:
  0.0 155.9 jit_solution(17392203688165639189)
XLA Ops:
  0.6 0.0 copy-start
  0.6 0.0 copy-start.9
  0.7 0.0 copy-start.10
  0.7 0.0 copy-start.11
  0.7 149.7 %shard_map.82 = (f32[2,2048,128]{2,1,0:T(8,128)}, f32[2048,128]{1,0:T(8,128)}, bf16[256,256]{1,0:T(8,128)(2,1)}, f32[512,384]{1,0:T(8,128)}, f32[128,128]{1,0:T(8,128)}, /*index=5*/f32[1,1]{1,0:T(1,128)}) custom-call(f32[2048,128]{1,0:T(8,128)} %refs_0_.1, f32[16,128]{1,0:T(8,128)} %bitcast.158, bf16[8,8,256,256]{3,2,1,0:T(8,128)(2,1)} %refs_2_.1, ...), custom_call_target="tpu_custom_call" | custom-call | tf_op jit(solution)/shard_map/pallas_call | solution.py:622
  151.0 0.0 copy-done
  151.1 0.0 copy-done.9
  151.1 0.0 copy-done.10
  151.1 0.0 copy-done.11
  151.1 4.7 %conditional.1 = ((f32[3,2048,128]{2,1,0:T(8,128)}, f32[512,384]{1,0:T(8,128)}, f32[128,128]{1,0:T(8,128)})) conditional(s32[]{:T(128)} %bitcast.50, (f32[2048]{0:T(1024)S(1)}, f32[2048,128]{1,0:T(8,128)S(1)}, s32[8,8]{1,0:T(8,128)S(1)}, s32[8,8]{1,0:T(8,128)S(1)}, bf16[8,8,256,256]{3,2,1,0:T(8,128)(2,1)}) %tuple.48, (f32[2,2048,128]{2,1,0:T(8,128)}, ...), branch_computations={%region_0.0_spmd, %region_3.7_spmd} | conditional | flops 11412555776 | bytes 290633440 | solution.py:731
  151.3 4.4 %branch_1_fun.1 = (f32[3,2048,128]{2,1,0:T(8,128)}, f32[512,384]{1,0:T(8,128)}, f32[128,128]{1,0:T(8,128)}) custom-call(f32[2,2048,128]{2,1,0:T(8,128)} %get-tuple-element.28.bases_ref, f32[2048,128]{1,0:T(8,128)} %get-tuple-element.29.rest_ref, bf16[256,256]{1,0:T(8,128)(2,1)} %get-tuple-element.30.inverse_ref, f32[512,384]{1,0:T(8,128)} %get-tuple-element.31.hess_ref, ...), custom_call_target="tpu_custom_call" | custom-call | tf_op jit(solution)/shard_map/cond/branch_1_fun/pallas_call | solution.py:706
Async XLA Ops:
  0.6 150.4 %copy-start = (f32[2048,128]{1,0:T(8,128)S(1)}, f32[2048,128]{1,0:T(8,128)}, u32[]{:S(2)}) copy-start(f32[2048,128]{1,0:T(8,128)} %refs_0_.1) | copy-start | bytes 3145732
  0.6 150.4 %copy-start.9 = (f32[2048]{0:T(1024)S(1)}, f32[2048]{0:T(1024)}, u32[]{:S(2)}) copy-start(f32[2048]{0:T(1024)} %param.13) | copy-start | bytes 24580
  0.7 150.4 %copy-start.10 = (s32[8,8]{1,0:T(8,128)S(1)}, s32[8,8]{1,0:T(8,128)}, u32[]{:S(2)}) copy-start(s32[8,8]{1,0:T(8,128)} %refs_3_.1) | copy-start | bytes 772
  0.7 150.4 %copy-start.11 = (s32[8,8]{1,0:T(8,128)S(1)}, s32[8,8]{1,0:T(8,128)}, u32[]{:S(2)}) copy-start(s32[8,8]{1,0:T(8,128)} %refs_4_.1) | copy-start | bytes 772

commit v4 on v3

--- a/solution.py
+++ b/solution.py
@@ -10,6 +10,7 @@
 W = 2
 STEPS = 3
 LIMIT = 16384.0
+TALL = 2
 F32 = jnp.float32
 BF16 = jnp.bfloat16
 MESH = pl.DeviceIdType.MESH
@@ -191,6 +192,7 @@
     rows = nb * bs
     stride = nb + 2 * W
     chunk = width // n_xy
+    tall = rows // TALL
     scale = 1.0 / (rows * n_span * n_band)
     s = lax.axis_index("span")
     z = lax.axis_index("band")
@@ -321,9 +323,14 @@
     load = pltpu.make_async_copy(blocks_ref, blk, blk_sem)
     load.start()
 
-    def accumulate(lefts, right):
-        for m, left in enumerate(lefts):
-            gram[m] = gram[m] + dot_rows(left, right)
+    def products(bases):
+        nm = bases + 1
+        for i in range(rows // tall):
+            here = pl.ds(i * tall, tall)
+            pair = both(mf[here, :])
+            lefts = jnp.concatenate([qs[m, here, :] for m in range(bases)] + [pair], axis=1)
+            value = dot_rows(lefts, pair).reshape(nm, 2 * width, 2 * width)
+            gram[:nm] = value if i == 0 else gram[:nm] + value
 
     def publish(t, nm):
         for m in range(nm):
@@ -333,81 +340,48 @@
         take = pl.ds(0, nm)
         par = t % 2
 
-        def first(who):
-            peer, device = who
+        def copy(stage, source, target, device):
             return pltpu.make_async_remote_copy(
-                src_ref=part.at[t, peer, take],
-                dst_ref=recv1.at[t, xy, take],
-                send_sem=send_sem.at[0, peer],
-                recv_sem=recv_sem.at[par, 0, xy],
+                src_ref=source,
+                dst_ref=target,
+                send_sem=send_sem.at[stage],
+                recv_sem=recv_sem.at[par, stage],
                 device_id=device,
                 device_id_type=MESH,
             )
 
-        def second(who):
-            peer, device = who
-            return pltpu.make_async_remote_copy(
-                src_ref=mid.at[t, take],
-                dst_ref=recv2.at[t, zc, take],
-                send_sem=send_sem.at[1, peer],
-                recv_sem=recv_sem.at[par, 1, zc],
-                device_id=device,
-                device_id_type=MESH,
-            )
-
-        def third(who):
-            peer, device = who
-            return pltpu.make_async_remote_copy(
-                src_ref=fin.at[t, take],
-                dst_ref=total.at[t, xy, take],
-                send_sem=send_sem.at[2, peer],
-                recv_sem=recv_sem.at[par, 2, xy],
-                device_id=device,
-                device_id_type=MESH,
-            )
-
-        def landed(buffer, stage, who, like):
-            peer, device = who
-            pltpu.make_async_remote_copy(
-                src_ref=like,
-                dst_ref=buffer.at[t, peer, take],
-                send_sem=send_sem.at[stage, peer],
-                recv_sem=recv_sem.at[par, stage, peer],
-                device_id=device,
-                device_id_type=MESH,
-            ).wait_recv()
-
-        def each(n, act):
-            def body(d, carry):
-                act(d)
-                return carry
-
-            lax.fori_loop(1, n, body, 0)
-
-        xy_far(lambda who: first(who).start())
+        def landed(stage, buffer, count):
+            pieces = buffer.at[t, pl.ds(0, count - 1), take]
+            copy(stage, pieces, pieces, (sibling, z)).wait_recv()
+
+        def left(stage, buffer, count):
+            pieces = buffer.at[t, pl.ds(0, count - 1), take]
+            copy(stage, pieces, pieces, (sibling, z)).wait_send()
+
+        xy_far(lambda who: copy(0, part.at[t, who[0], take], recv1.at[t, xy, take], who[1]).start())
         recv1[t, xy, :nm] = part[t, xy, :nm]
         if meanwhile is not None:
             meanwhile()
-        each(n_xy, lambda d: landed(recv1, 0, xy_peer(d), mid.at[t, take]))
+        landed(0, recv1, n_xy)
         value = recv1[t, 0, :nm]
         for i in range(1, n_xy):
             value = value + recv1[t, i, :nm]
         mid[t, :nm] = value
-        zc_far(lambda who: second(who).start())
+        zc_far(lambda who: copy(1, mid.at[t, take], recv2.at[t, zc, take], who[1]).start())
         recv2[t, zc, :nm] = value
-        each(n_zc, lambda d: landed(recv2, 1, zc_peer(d), mid.at[t, take]))
+        landed(1, recv2, n_zc)
         value = recv2[t, 0, :nm]
         for i in range(1, n_zc):
             value = value + recv2[t, i, :nm]
         fin[t, :nm] = value
-        xy_far(lambda who: third(who).start())
+        xy_far(lambda who: copy(2, fin.at[t, take], total.at[t, xy, take], who[1]).start())
         total[t, xy, :nm] = value
-        each(n_xy, lambda d: landed(total, 2, xy_peer(d), fin.at[t, take]))
+        landed(2, total, n_xy)
 
         def sent():
-            each(n_xy, lambda d: first(xy_peer(d)).wait_send())
-            each(n_zc, lambda d: second(zc_peer(d)).wait_send())
-            each(n_xy, lambda d: third(xy_peer(d)).wait_send())
+            left(0, recv1, n_xy)
+            left(1, recv2, n_zc)
+            left(2, total, n_xy)
 
         return [total[t, :, m].reshape(width, width) for m in range(nm)], sent
 
@@ -507,24 +481,15 @@
             form(i)
             return carry
 
-        lax.fori_loop(0, 2 * W, ends, 0)
+        lax.fori_loop(0, 2 * W, ends, 0, unroll=True)
         send(0, 1, 2, 3)
-        lax.fori_loop(W, nb - W, middle, 0)
+        lax.fori_loop(W, nb - W, middle, 0, unroll=True)
         send(4, 5)
 
     cond[...] = jnp.zeros_like(cond)
     hess_ref[...] = jnp.zeros_like(hess_ref)
-    gram[0] = jnp.zeros_like(gram[0])
-
-    def start_part(i, carry):
-        here = pl.ds(pl.multiple_of(i * bs, bs), bs)
-        value = start_ref[here, :]
-        mf[here, :] = value
-        pair = both(value)
-        accumulate([pair], pair)
-        return carry
-
-    lax.fori_loop(0, nb, start_part, 0)
+    mf[...] = start_ref[...]
+    products(0)
     publish(0, 1)
     pl.semaphore_wait(barrier, n_xy + n_zc - 2 + has_beyond.astype(jnp.int32))
 
@@ -549,8 +514,6 @@
         if j > 0:
             pltpu.make_async_copy(qf.at[j], bases_ref.at[j - 1], out_sem.at[j - 1]).start()
         sent()
-        for m in range(j + 2):
-            gram[m] = jnp.zeros_like(gram[m])
         arrived(3)
         send(6)
         arrived(2)
@@ -568,11 +531,10 @@
                 at = (spans_ref[i, k] + 1) * stride + i + W + cols_ref[i, k]
                 acc = acc + dot(blk[i, k], ext[at])
             mf[here, :] = acc
-            pair = both(acc)
-            accumulate([qs[m, here, :] for m in range(j + 1)] + [pair], pair)
             return carry
 
-        lax.fori_loop(0, nb, block_row, 0)
+        lax.fori_loop(0, nb, block_row, 0, unroll=2)
+        products(j + 1)
         sent_halo(6, 7, 8, 9)
         publish(j + 1, j + 2)
         sums, sent = all_reduce(j + 1, j + 2, lambda: sent_halo(0, 1, 2, 3, 4, 5))
@@ -652,8 +614,8 @@
             pltpu.VMEM((nm, nm, chunk, width), F32),
             pltpu.VMEM((nm, n_xy, nm, chunk, width), F32),
             pltpu.VMEM((1, width), F32),
-            pltpu.SemaphoreType.DMA((3, max(n_xy, n_zc))),
-            pltpu.SemaphoreType.DMA((2, 3, max(n_xy, n_zc))),
+            pltpu.SemaphoreType.DMA((3,)),
+            pltpu.SemaphoreType.DMA((2, 3)),
             pltpu.SemaphoreType.DMA((10,)),
             pltpu.SemaphoreType.DMA((10,)),
             pltpu.SemaphoreType.DMA,

time: 156 us -> 148 us (0.949)
  Pallas kernels: 154 us -> 147 us
    pallas_call x1, Pallas kernels: 150 us -> 142 us  [short_form(): pl.pallas_call(body, out_shape=(jax.ShapeDtypeStruct((STEPS - 1, rows, wi...]
where the time goes in v4:
time: 148 us
  Pallas kernels  147 us (99%)
  between operations  1.5 us (1%)
    pallas_call x1, Pallas kernels, short_form(): pl.pallas_call(body, out_shape=(jax.ShapeDtypeStruct((STEPS - 1, rows, wi...  142 us
    pallas_call x1, Pallas kernels, finish(): pl.pallas_call(body, out_shape=(jax.ShapeDtypeStruct((before + 1, rows, w...  4.43 us

profile of v4, /device:TPU:1, one launch (start us, length us, event | category | flops | bytes accessed | tf_op | source)
XLA Modules:
  0.0 148.3 jit_solution(13042207674821416124)
XLA Ops:
  0.6 0.0 copy-start
  0.6 0.0 copy-start.9
  0.7 0.0 copy-start.10
  0.7 0.0 copy-start.11
  0.7 142.1 %shard_map.82 = (f32[2,2048,128]{2,1,0:T(8,128)}, f32[2048,128]{1,0:T(8,128)}, bf16[256,256]{1,0:T(8,128)(2,1)}, f32[512,384]{1,0:T(8,128)}, f32[128,128]{1,0:T(8,128)}, /*index=5*/f32[1,1]{1,0:T(1,128)}) custom-call(f32[2048,128]{1,0:T(8,128)} %refs_0_.1, f32[16,128]{1,0:T(8,128)} %bitcast.158, bf16[8,8,256,256]{3,2,1,0:T(8,128)(2,1)} %refs_2_.1, ...), custom_call_target="tpu_custom_call" | custom-call | tf_op jit(solution)/shard_map/pallas_call | solution.py:584
  143.4 0.0 copy-done
  143.4 0.0 copy-done.9
  143.4 0.0 copy-done.10
  143.4 0.0 copy-done.11
  143.5 4.7 %conditional.1 = ((f32[3,2048,128]{2,1,0:T(8,128)}, f32[512,384]{1,0:T(8,128)}, f32[128,128]{1,0:T(8,128)})) conditional(s32[]{:T(128)} %bitcast.50, (f32[2048]{0:T(1024)S(1)}, f32[2048,128]{1,0:T(8,128)S(1)}, s32[8,8]{1,0:T(8,128)S(1)}, s32[8,8]{1,0:T(8,128)S(1)}, bf16[8,8,256,256]{3,2,1,0:T(8,128)(2,1)}) %tuple.48, (f32[2,2048,128]{2,1,0:T(8,128)}, ...), branch_computations={%region_0.0_spmd, %region_3.7_spmd} | conditional | flops 11412555776 | bytes 290633440 | solution.py:693
  143.7 4.4 %branch_1_fun.1 = (f32[3,2048,128]{2,1,0:T(8,128)}, f32[512,384]{1,0:T(8,128)}, f32[128,128]{1,0:T(8,128)}) custom-call(f32[2,2048,128]{2,1,0:T(8,128)} %get-tuple-element.28.bases_ref, f32[2048,128]{1,0:T(8,128)} %get-tuple-element.29.rest_ref, bf16[256,256]{1,0:T(8,128)(2,1)} %get-tuple-element.30.inverse_ref, f32[512,384]{1,0:T(8,128)} %get-tuple-element.31.hess_ref, ...), custom_call_target="tpu_custom_call" | custom-call | tf_op jit(solution)/shard_map/cond/branch_1_fun/pallas_call | solution.py:668
Async XLA Ops:
  0.6 142.8 %copy-start = (f32[2048,128]{1,0:T(8,128)S(1)}, f32[2048,128]{1,0:T(8,128)}, u32[]{:S(2)}) copy-start(f32[2048,128]{1,0:T(8,128)} %refs_0_.1) | copy-start | bytes 3145732
  0.6 142.8 %copy-start.9 = (f32[2048]{0:T(1024)S(1)}, f32[2048]{0:T(1024)}, u32[]{:S(2)}) copy-start(f32[2048]{0:T(1024)} %param.13) | copy-start | bytes 24580
  0.7 142.8 %copy-start.10 = (s32[8,8]{1,0:T(8,128)S(1)}, s32[8,8]{1,0:T(8,128)}, u32[]{:S(2)}) copy-start(s32[8,8]{1,0:T(8,128)} %refs_3_.1) | copy-start | bytes 772
  0.7 142.8 %copy-start.11 = (s32[8,8]{1,0:T(8,128)S(1)}, s32[8,8]{1,0:T(8,128)}, u32[]{:S(2)}) copy-start(s32[8,8]{1,0:T(8,128)} %refs_4_.1) | copy-start | bytes 772

commit v5 on v4

--- a/solution.py
+++ b/solution.py
@@ -160,6 +160,8 @@
     hess_ref,
     first_ref,
     flag_ref,
+    hess,
+    first,
     blk,
     ext,
     qf,
@@ -304,6 +306,9 @@
             def _():
                 move(n, source, here, count, device).wait_recv()
 
+    first_load = pltpu.make_async_copy(start_ref, mf, blk_sem.at[0])
+    first_load.start()
+    load = pltpu.make_async_copy(blocks_ref, blk, blk_sem.at[1])
     barrier = pltpu.get_barrier_semaphore()
 
     def greet(peer_of):
@@ -320,7 +325,6 @@
     def _():
         pl.semaphore_signal(barrier, inc=1, device_id=(beyond, z), device_id_type=MESH)
 
-    load = pltpu.make_async_copy(blocks_ref, blk, blk_sem)
     load.start()
 
     def products(bases):
@@ -394,9 +398,10 @@
         )
         work[:, w:] = jnp.where(eye, 1.0, 0.0).astype(F32)
         row = lax.broadcasted_iota(jnp.int32, tile, 0)
-        lane = lax.broadcasted_iota(jnp.int32, tile, 1)
+        place = lax.broadcasted_iota(jnp.int32, (16, w), 0)
+        lane = lax.broadcasted_iota(jnp.int32, (16, w), 1)
         lanes = lax.broadcasted_iota(jnp.int32, (w, w), 1)
-        within, group = lax.rem(lanes, 8), lanes // 8
+        within, group = lax.rem(lanes, 16), lanes // 16
         firsts = (group == 0) | (group == 1) | (group == 4)
         seconds = (group == 2) | (group == 3)
         thirds = group == 5
@@ -407,27 +412,16 @@
                 out = jnp.where(row == j, lines[j], out)
             return out
 
-        def panel(p, carry):
-            k0 = pl.multiple_of(p * 8, 8)
-            pivot = work[pl.ds(k0, 8), :w]
-            for j in range(8):
-                spread[j] = jnp.take_along_axis(pivot, jnp.broadcast_to(k0 + j, tile), axis=1)
-            spread[8] = pivot
-            spread[9] = work[pl.ds(k0, 8), w:]
-            columns = jnp.take_along_axis(work[:, :w], k0 + within, axis=1)
-            a1 = rounded(columns)
-            a2 = rounded(columns - a1)
-            a3 = columns - a1 - a2
-            left = jnp.where(firsts, a1, jnp.where(seconds, a2, jnp.where(thirds, a3, 0.0)))
-            left = left.astype(BF16)[:, :48]
-
-            def line(n, i):
-                return jnp.broadcast_to(spread[n, pl.ds(i, 1), :], tile)
-
-            a = [[line(j, i) if i >= j else None for j in range(8)] for i in range(8)]
-            heads = [line(8, i) for i in range(8)]
-            tails = [line(9, i) for i in range(8)]
-            beside(p)
+        def line(n, i):
+            return jnp.broadcast_to(spread[n, pl.ds(i, 1), :], tile)
+
+        def lines(n):
+            return [line(n, i) for i in range(8)]
+
+        def triangle(n):
+            return [[line(n + j, i) if i >= j else None for j in range(8)] for i in range(8)]
+
+        def eliminate(a, heads, tails, below):
             by = [None] * 8
             for j in range(8):
                 by[j] = lax.rsqrt(a[j][j])
@@ -435,20 +429,75 @@
                 tails[j] = tails[j] * by[j]
                 for i in range(j + 1, 8):
                     a[i][j] = a[i][j] * by[j]
+                if below:
+                    below[j] = below[j] * by[j]
                 for i in range(j + 1, 8):
                     for m in range(j + 1, i + 1):
                         a[i][m] = a[i][m] - a[i][j] * a[m][j]
                     heads[i] = heads[i] - a[i][j] * heads[j]
                     tails[i] = tails[i] - a[i][j] * tails[j]
-            fac[pl.ds(k0, 8), :] = jnp.where(lane >= k0 + row, assemble(heads), 0.0)
-            inv[pl.ds(k0, 8), :] = assemble(tails)
+                    if below:
+                        below[i] = below[i] - below[j] * a[i][j]
+            return by
+
+        def substitute(a, by, heads, tails):
             for j in range(7, -1, -1):
                 heads[j] = heads[j] * by[j]
                 tails[j] = tails[j] * by[j]
                 for i in range(j):
                     heads[i] = heads[i] - a[j][i] * heads[j]
                     tails[i] = tails[i] - a[j][i] * tails[j]
-            right = jnp.concatenate([assemble(heads), assemble(tails)], axis=1)
+
+        def panel(p, carry):
+            k0 = pl.multiple_of(p * 16, 16)
+            upper = work[pl.ds(k0, 8), :w]
+            lower = work[pl.ds(k0 + 8, 8), :w]
+
+            def column(rows_of, j):
+                return jnp.take_along_axis(rows_of, jnp.broadcast_to(k0 + j, tile), axis=1)
+
+            for j in range(8):
+                spread[j] = column(upper, j)
+            below = [column(lower, j) for j in range(8)]
+            block = [column(lower, 8 + j) for j in range(8)]
+            spread[8] = upper
+            spread[9] = work[pl.ds(k0, 8), w:]
+            columns = jnp.take_along_axis(work[:, :w], k0 + within, axis=1)
+            a1 = rounded(columns)
+            a2 = rounded(columns - a1)
+            a3 = columns - a1 - a2
+            left = jnp.where(firsts, a1, jnp.where(seconds, a2, jnp.where(thirds, a3, 0.0)))
+            left = left.astype(BF16)[:, :96]
+            beside(p)
+            a, heads, tails = triangle(0), lines(8), lines(9)
+            by = eliminate(a, heads, tails, below)
+            lower_tail = work[pl.ds(k0 + 8, 8), w:]
+            for m in range(8):
+                spread[10 + m] = below[m]
+                lower = lower - below[m] * heads[m]
+                lower_tail = lower_tail - below[m] * tails[m]
+            cross = [[line(10 + m, i) for m in range(8)] for i in range(8)]
+            for j in range(8):
+                for m in range(8):
+                    block[j] = block[j] - below[m] * cross[j][m]
+                spread[18 + j] = block[j]
+            spread[26] = lower
+            spread[27] = lower_tail
+            b, heads2, tails2 = triangle(18), lines(26), lines(27)
+            by2 = eliminate(b, heads2, tails2, None)
+
+            def stacked(first, second):
+                return jnp.concatenate([assemble(first), assemble(second)], axis=0)
+
+            fac[pl.ds(k0, 16), :] = jnp.where(lane >= k0 + place, stacked(heads, heads2), 0.0)
+            inv[pl.ds(k0, 16), :] = stacked(tails, tails2)
+            substitute(b, by2, heads2, tails2)
+            for j in range(8):
+                for i in range(7, -1, -1):
+                    heads[j] = heads[j] - cross[i][j] * heads2[i]
+                    tails[j] = tails[j] - cross[i][j] * tails2[i]
+            substitute(a, by, heads, tails)
+            right = jnp.concatenate([stacked(heads, heads2), stacked(tails, tails2)], axis=1)
             b1 = rounded(right)
             b2 = rounded(right - b1)
             b3 = right - b1 - b2
@@ -456,7 +505,7 @@
             work[...] = work[...] - dot(left, rights)
             return carry
 
-        lax.fori_loop(0, w // 8, panel, 0)
+        lax.fori_loop(0, w // 16, panel, 0)
         inverse = inv[...]
         lb[...] = square(inverse.T)
         diag = jnp.sum(jnp.where(eye, carry_gram[0], 0.0), axis=0, keepdims=True)
@@ -487,14 +536,14 @@
         send(4, 5)
 
     cond[...] = jnp.zeros_like(cond)
-    hess_ref[...] = jnp.zeros_like(hess_ref)
-    mf[...] = start_ref[...]
+    first_load.wait()
     products(0)
     publish(0, 1)
     pl.semaphore_wait(barrier, n_xy + n_zc - 2 + has_beyond.astype(jnp.int32))
 
     def expand_diag():
         ext[...] = jnp.zeros_like(ext)
+        hess[...] = jnp.zeros_like(hess)
 
         def body(c, carry):
             line = jnp.broadcast_to(diag_ref[pl.ds(c, 1), :], (width, width))
@@ -506,7 +555,12 @@
     (matrix,), sent = all_reduce(0, 1, expand_diag)
     carry_gram[0] = matrix
     factor(matrix, lambda p: None)
-    first_ref[...] = fac[...]
+    first[...] = fac[...]
+    first_out = pltpu.make_async_copy(first, first_ref, out_sem.at[STEPS + 3])
+    first_out.start()
+    cut = rows - 2 * (rows // (width // 16))
+    early_rows, late_rows = pl.ds(0, cut), pl.ds(cut, rows - cut)
+    early = pltpu.make_async_copy(mf.at[early_rows], rest_ref.at[early_rows], out_sem.at[STEPS - 1])
     load.wait()
 
     for j in range(STEPS):
@@ -541,28 +595,43 @@
         matrix = sums[j + 1]
         carry_gram[0] = matrix
         for i in range(j + 1):
-            hess_ref[i * width : (i + 1) * width, j * width : (j + 1) * width] = sums[i]
+            hess[i * width : (i + 1) * width, j * width : (j + 1) * width] = sums[i]
             hb[i] = square(sums[i])
-            matrix = matrix - dot_rows(sums[i], sums[i], HIGHEST)
+
+        tallest = jnp.concatenate(sums[: j + 1], axis=0)
+        matrix = matrix - dot_rows(tallest, tallest, HIGHEST)
+        share = rows // (width // 16)
 
         def residual_part(p, j=j):
-            here = pl.ds(pl.multiple_of(p * (rows // (width // 8)), rows // (width // 8)), rows // (width // 8))
+            here = pl.ds(pl.multiple_of(p * share, share), share)
             value = mf[here, :]
             for i in range(j + 1):
                 value = value - halves(dot(qs[i, here, :], hb[i]))
             mf[here, :] = value
+            if j == STEPS - 1:
+
+                @pl.when(p == width // 16 - 2)
+                def _():
+                    early.start()
 
         factor(matrix, residual_part)
-        hess_ref[(j + 1) * width : (j + 2) * width, j * width : (j + 1) * width] = fac[...]
-
-    last = pltpu.make_async_copy(mf, rest_ref, out_sem.at[STEPS - 1])
-    last.start()
+        hess[(j + 1) * width : (j + 2) * width, j * width : (j + 1) * width] = fac[...]
+
+    ends = [
+        pltpu.make_async_copy(mf.at[late_rows], rest_ref.at[late_rows], out_sem.at[STEPS]),
+        pltpu.make_async_copy(lb, inverse_ref, out_sem.at[STEPS + 1]),
+        pltpu.make_async_copy(hess, hess_ref, out_sem.at[STEPS + 2]),
+    ]
+    for copy in ends:
+        copy.start()
     sent()
-    inverse_ref[...] = lb[...]
     flag_ref[0, 0] = jnp.sum(cond[...])
     for j in range(1, STEPS):
         pltpu.make_async_copy(qf.at[j], bases_ref.at[j - 1], out_sem.at[j - 1]).wait()
-    last.wait()
+    early.wait()
+    first_out.wait()
+    for copy in ends:
+        copy.wait()
 
 
 def short_form(start_block, diagonal, blocks, span_offsets, col_offsets):
@@ -591,9 +660,11 @@
             jax.ShapeDtypeStruct((width, width), F32),
             jax.ShapeDtypeStruct((1, 1), F32),
         ),
-        in_specs=[vmem, vmem, anywhere, smem, smem],
-        out_specs=(anywhere, anywhere, vmem, vmem, vmem, smem),
+        in_specs=[anywhere, vmem, anywhere, smem, smem],
+        out_specs=(anywhere,) * 5 + (smem,),
         scratch_shapes=[
+            pltpu.VMEM(((STEPS + 1) * width, STEPS * width), F32),
+            pltpu.VMEM((width, width), F32),
             pltpu.VMEM((nb, kc, bs, bs), BF16),
             pltpu.VMEM((3 * stride, bs, width), BF16),
             pltpu.VMEM((STEPS, rows, width), F32),
@@ -604,7 +675,7 @@
             pltpu.VMEM((width, 2 * width), F32),
             pltpu.VMEM((width, width), F32),
             pltpu.VMEM((width, width), F32),
-            pltpu.VMEM((10, 8, width), F32),
+            pltpu.VMEM((28, 8, width), F32),
             pltpu.VMEM((STEPS, 2 * width, 2 * width), BF16),
             pltpu.VMEM((2 * width, 2 * width), BF16),
             pltpu.VMEM((nm, n_xy, nm, chunk, width), F32),
@@ -618,8 +689,8 @@
             pltpu.SemaphoreType.DMA((2, 3)),
             pltpu.SemaphoreType.DMA((10,)),
             pltpu.SemaphoreType.DMA((10,)),
-            pltpu.SemaphoreType.DMA,
-            pltpu.SemaphoreType.DMA((STEPS,)),
+            pltpu.SemaphoreType.DMA((2,)),
+            pltpu.SemaphoreType.DMA((STEPS + 4,)),
         ],
         compiler_params=pltpu.CompilerParams(
             collective_id=0, has_side_effects=True, vmem_limit_bytes=48 * 1024 * 1024

time: 148 us -> 143 us (0.966)
  Pallas kernels: 147 us -> 141 us
    pallas_call x1, Pallas kernels: 142 us -> 136 us  [short_form(): pl.pallas_call(body, out_shape=(jax.ShapeDtypeStruct((STEPS - 1, rows, wi...]
where the time goes in v5:
time: 143 us
  Pallas kernels  141 us (99%)
  between operations  1.5 us (1%)
    pallas_call x1, Pallas kernels, short_form(): pl.pallas_call(body, out_shape=(jax.ShapeDtypeStruct((STEPS - 1, rows, wi...  136 us
    pallas_call x1, Pallas kernels, finish(): pl.pallas_call(body, out_shape=(jax.ShapeDtypeStruct((before + 1, rows, w...  4.43 us

profile of v5, /device:TPU:1, one launch (start us, length us, event | category | flops | bytes accessed | tf_op | source)
XLA Modules:
  0.0 142.5 jit_solution(13482392466195178671)
XLA Ops:
  0.6 0.0 copy-start
  0.6 0.0 copy-start.9
  0.7 0.0 copy-start.10
  0.7 0.0 copy-start.11
  0.7 136.3 %shard_map.82 = (f32[2,2048,128]{2,1,0:T(8,128)}, f32[2048,128]{1,0:T(8,128)}, bf16[256,256]{1,0:T(8,128)(2,1)}, f32[512,384]{1,0:T(8,128)}, f32[128,128]{1,0:T(8,128)}, /*index=5*/f32[1,1]{1,0:T(1,128)}) custom-call(f32[2048,128]{1,0:T(8,128)} %refs_0_.1, f32[16,128]{1,0:T(8,128)} %bitcast.158, bf16[8,8,256,256]{3,2,1,0:T(8,128)(2,1)} %refs_2_.1, ...), custom_call_target="tpu_custom_call" | custom-call | tf_op jit(solution)/shard_map/pallas_call | solution.py:653
  137.6 0.0 copy-done
  137.6 0.0 copy-done.9
  137.6 0.0 copy-done.10
  137.7 0.0 copy-done.11
  137.7 4.7 %conditional.1 = ((f32[3,2048,128]{2,1,0:T(8,128)}, f32[512,384]{1,0:T(8,128)}, f32[128,128]{1,0:T(8,128)})) conditional(s32[]{:T(128)} %bitcast.50, (f32[2048]{0:T(1024)S(1)}, f32[2048,128]{1,0:T(8,128)S(1)}, s32[8,8]{1,0:T(8,128)S(1)}, s32[8,8]{1,0:T(8,128)S(1)}, bf16[8,8,256,256]{3,2,1,0:T(8,128)(2,1)}) %tuple.48, (f32[2,2048,128]{2,1,0:T(8,128)}, ...), branch_computations={%region_0.0_spmd, %region_3.7_spmd} | conditional | flops 11412555776 | bytes 290633440 | solution.py:764
  137.9 4.4 %branch_1_fun.1 = (f32[3,2048,128]{2,1,0:T(8,128)}, f32[512,384]{1,0:T(8,128)}, f32[128,128]{1,0:T(8,128)}) custom-call(f32[2,2048,128]{2,1,0:T(8,128)} %get-tuple-element.28.bases_ref, f32[2048,128]{1,0:T(8,128)} %get-tuple-element.29.rest_ref, bf16[256,256]{1,0:T(8,128)(2,1)} %get-tuple-element.30.inverse_ref, f32[512,384]{1,0:T(8,128)} %get-tuple-element.31.hess_ref, ...), custom_call_target="tpu_custom_call" | custom-call | tf_op jit(solution)/shard_map/cond/branch_1_fun/pallas_call | solution.py:739
Async XLA Ops:
  0.6 137.0 %copy-start = (f32[2048,128]{1,0:T(8,128)S(1)}, f32[2048,128]{1,0:T(8,128)}, u32[]{:S(2)}) copy-start(f32[2048,128]{1,0:T(8,128)} %refs_0_.1) | copy-start | bytes 3145732
  0.6 137.0 %copy-start.9 = (f32[2048]{0:T(1024)S(1)}, f32[2048]{0:T(1024)}, u32[]{:S(2)}) copy-start(f32[2048]{0:T(1024)} %param.13) | copy-start | bytes 24580
  0.7 137.0 %copy-start.10 = (s32[8,8]{1,0:T(8,128)S(1)}, s32[8,8]{1,0:T(8,128)}, u32[]{:S(2)}) copy-start(s32[8,8]{1,0:T(8,128)} %refs_3_.1) | copy-start | bytes 772
  0.7 137.0 %copy-start.11 = (s32[8,8]{1,0:T(8,128)S(1)}, s32[8,8]{1,0:T(8,128)}, u32[]{:S(2)}) copy-start(s32[8,8]{1,0:T(8,128)} %refs_4_.1) | copy-start | bytes 772

commit v6 on v5

--- a/solution.py
+++ b/solution.py
@@ -10,7 +10,6 @@
 W = 2
 STEPS = 3
 LIMIT = 16384.0
-TALL = 2
 F32 = jnp.float32
 BF16 = jnp.bfloat16
 MESH = pl.DeviceIdType.MESH
@@ -168,7 +167,6 @@
     qs,
     mf,
     dg,
-    gram,
     work,
     fac,
     inv,
@@ -194,7 +192,6 @@
     rows = nb * bs
     stride = nb + 2 * W
     chunk = width // n_xy
-    tall = rows // TALL
     scale = 1.0 / (rows * n_span * n_band)
     s = lax.axis_index("span")
     z = lax.axis_index("band")
@@ -327,18 +324,12 @@
 
     load.start()
 
-    def products(bases):
-        nm = bases + 1
-        for i in range(rows // tall):
-            here = pl.ds(i * tall, tall)
-            pair = both(mf[here, :])
-            lefts = jnp.concatenate([qs[m, here, :] for m in range(bases)] + [pair], axis=1)
-            value = dot_rows(lefts, pair).reshape(nm, 2 * width, 2 * width)
-            gram[:nm] = value if i == 0 else gram[:nm] + value
-
-    def publish(t, nm):
-        for m in range(nm):
-            part[t, :, m] = (quarters(gram[m]) * scale).reshape(n_xy, chunk, width)
+    def publish(t, bases):
+        pair = both(mf[...])
+        lefts = jnp.concatenate([qs[m] for m in range(bases)] + [pair], axis=1)
+        value = dot_rows(lefts, pair).reshape(bases + 1, 2 * width, 2 * width)
+        for m in range(bases + 1):
+            part[t, :, m] = (quarters(value[m]) * scale).reshape(n_xy, chunk, width)
 
     def all_reduce(t, nm, meanwhile=None):
         take = pl.ds(0, nm)
@@ -537,8 +528,7 @@
 
     cond[...] = jnp.zeros_like(cond)
     first_load.wait()
-    products(0)
-    publish(0, 1)
+    publish(0, 0)
     pl.semaphore_wait(barrier, n_xy + n_zc - 2 + has_beyond.astype(jnp.int32))
 
     def expand_diag():
@@ -587,10 +577,9 @@
             mf[here, :] = acc
             return carry
 
-        lax.fori_loop(0, nb, block_row, 0, unroll=2)
-        products(j + 1)
+        lax.fori_loop(0, nb, block_row, 0, unroll=4)
         sent_halo(6, 7, 8, 9)
-        publish(j + 1, j + 2)
+        publish(j + 1, j + 1)
         sums, sent = all_reduce(j + 1, j + 2, lambda: sent_halo(0, 1, 2, 3, 4, 5))
         matrix = sums[j + 1]
         carry_gram[0] = matrix
@@ -671,7 +660,6 @@
             pltpu.VMEM((STEPS, rows, 2 * width), BF16),
             pltpu.VMEM((rows, width), F32),
             pltpu.VMEM((rows, width), F32),
-            pltpu.VMEM((nm, 2 * width, 2 * width), F32),
             pltpu.VMEM((width, 2 * width), F32),
             pltpu.VMEM((width, width), F32),
             pltpu.VMEM((width, width), F32),
@@ -706,7 +694,9 @@
     def body(
         bases_ref, rest_ref, inverse_ref, hess_ref, first_ref, bases_to, hess_to, first_to, *scratch
     ):
-        q, r, out, hess, first, in_sem, out_sem = scratch
+        inv, q, r, out, hess, first, in_sem, out_sem = scratch
+        fetch = pltpu.make_async_copy(inverse_ref, inv, in_sem.at[chunks + before + 2])
+        fetch.start()
         parts = [pl.ds(i * chunk, chunk) for i in range(chunks)]
         loads = [
             pltpu.make_async_copy(rest_ref.at[here], r.at[here], in_sem.at[i])
@@ -719,9 +709,10 @@
         for load in loads:
             load.start()
         stores = []
+        fetch.wait()
         for i, here in enumerate(parts):
             loads[i].wait()
-            out[here, :] = halves(dot(both(r[here, :]), inverse_ref[...]))
+            out[here, :] = halves(dot(both(r[here, :]), inv[...]))
             stores.append(
                 pltpu.make_async_copy(out.at[here], bases_to.at[before, here], out_sem.at[i])
             )
@@ -735,7 +726,6 @@
             store.wait()
 
     anywhere = pl.BlockSpec(memory_space=pl.ANY)
-    vmem = pl.BlockSpec(memory_space=pltpu.VMEM)
     return pl.pallas_call(
         body,
         out_shape=(
@@ -743,15 +733,16 @@
             jax.ShapeDtypeStruct(hessenberg.shape, F32),
             jax.ShapeDtypeStruct(r_first.shape, F32),
         ),
-        in_specs=[anywhere, anywhere, vmem, anywhere, anywhere],
+        in_specs=[anywhere] * 5,
         out_specs=(anywhere,) * 3,
         scratch_shapes=[
+            pltpu.VMEM(inverse.shape, inverse.dtype),
             pltpu.VMEM(bases.shape, F32),
             pltpu.VMEM((rows, width), F32),
             pltpu.VMEM((rows, width), F32),
             pltpu.VMEM(hessenberg.shape, F32),
             pltpu.VMEM(r_first.shape, F32),
-            pltpu.SemaphoreType.DMA((chunks + before + 2,)),
+            pltpu.SemaphoreType.DMA((chunks + before + 3,)),
             pltpu.SemaphoreType.DMA((chunks + before + 2,)),
         ],
         compiler_params=pltpu.CompilerParams(vmem_limit_bytes=16 * 1024 * 1024),

time: 143 us -> 141 us (0.986)
  Pallas kernels: 141 us -> 139 us
where the time goes in v6:
time: 141 us
  Pallas kernels  139 us (99%)
  between operations  1.52 us (1%)
    pallas_call x1, Pallas kernels, short_form(): pl.pallas_call(body, out_shape=(jax.ShapeDtypeStruct((STEPS - 1, rows, wi...  136 us
    pallas_call x1, Pallas kernels, finish(): pl.pallas_call(body, out_shape=(jax.ShapeDtypeStruct((before + 1, rows, w...  3.6 us

profile of v6, /device:TPU:1, one launch (start us, length us, event | category | flops | bytes accessed | tf_op | source)
XLA Modules:
  0.0 141.3 jit_solution(2255400894240978178)
XLA Ops:
  0.6 0.0 copy-start
  0.6 0.0 copy-start.9
  0.7 0.0 copy-start.10
  0.7 0.0 copy-start.11
  0.7 135.9 %shard_map.82 = (f32[2,2048,128]{2,1,0:T(8,128)}, f32[2048,128]{1,0:T(8,128)}, bf16[256,256]{1,0:T(8,128)(2,1)}, f32[512,384]{1,0:T(8,128)}, f32[128,128]{1,0:T(8,128)}, /*index=5*/f32[1,1]{1,0:T(1,128)}) custom-call(f32[2048,128]{1,0:T(8,128)} %refs_0_.1, f32[16,128]{1,0:T(8,128)} %bitcast.158, bf16[8,8,256,256]{3,2,1,0:T(8,128)(2,1)} %refs_2_.1, ...), custom_call_target="tpu_custom_call" | custom-call | tf_op jit(solution)/shard_map/pallas_call | solution.py:642
  137.2 0.0 copy-done
  137.2 0.0 copy-done.9
  137.2 0.0 copy-done.10
  137.2 0.0 copy-done.11
  137.2 3.9 %conditional.1 = ((f32[3,2048,128]{2,1,0:T(8,128)}, f32[512,384]{1,0:T(8,128)}, f32[128,128]{1,0:T(8,128)})) conditional(s32[]{:T(128)} %bitcast.50, (f32[2048]{0:T(1024)S(1)}, f32[2048,128]{1,0:T(8,128)S(1)}, s32[8,8]{1,0:T(8,128)S(1)}, s32[8,8]{1,0:T(8,128)S(1)}, bf16[8,8,256,256]{3,2,1,0:T(8,128)(2,1)}) %tuple.48, (f32[2,2048,128]{2,1,0:T(8,128)}, ...), branch_computations={%region_0.0_spmd, %region_3.7_spmd} | conditional | flops 11412555776 | bytes 290633440 | solution.py:755
  137.5 3.6 %branch_1_fun.1 = (f32[3,2048,128]{2,1,0:T(8,128)}, f32[512,384]{1,0:T(8,128)}, f32[128,128]{1,0:T(8,128)}) custom-call(f32[2,2048,128]{2,1,0:T(8,128)} %get-tuple-element.28.bases_ref, f32[2048,128]{1,0:T(8,128)} %get-tuple-element.29.rest_ref, bf16[256,256]{1,0:T(8,128)(2,1)} %get-tuple-element.30.inverse_ref, f32[512,384]{1,0:T(8,128)} %get-tuple-element.31.hess_ref, ...), custom_call_target="tpu_custom_call" | custom-call | tf_op jit(solution)/shard_map/cond/branch_1_fun/pallas_call | solution.py:729
Async XLA Ops:
  0.6 136.5 %copy-start = (f32[2048,128]{1,0:T(8,128)S(1)}, f32[2048,128]{1,0:T(8,128)}, u32[]{:S(2)}) copy-start(f32[2048,128]{1,0:T(8,128)} %refs_0_.1) | copy-start | bytes 3145732
  0.6 136.5 %copy-start.9 = (f32[2048]{0:T(1024)S(1)}, f32[2048]{0:T(1024)}, u32[]{:S(2)}) copy-start(f32[2048]{0:T(1024)} %param.13) | copy-start | bytes 24580
  0.7 136.5 %copy-start.10 = (s32[8,8]{1,0:T(8,128)S(1)}, s32[8,8]{1,0:T(8,128)}, u32[]{:S(2)}) copy-start(s32[8,8]{1,0:T(8,128)} %refs_3_.1) | copy-start | bytes 772
  0.7 136.5 %copy-start.11 = (s32[8,8]{1,0:T(8,128)S(1)}, s32[8,8]{1,0:T(8,128)}, u32[]{:S(2)}) copy-start(s32[8,8]{1,0:T(8,128)} %refs_4_.1) | copy-start | bytes 772
